TPU v7x, 32 devices: a whole 2x2x4 slice. The times are simulated.
32 devices in a mesh: dp: 8 (over z, x), section: 4 (over y, core).
Axes of the slice: x: 2, y: 2, z: 4, core: 2. Of those that a mesh axis runs over, the one named last changes fastest.
Arguments:
- tokens: bfloat16 [24576, 768], P(('dp', 'section')), may hold values from -6 to 6
- counts: int32 [16, 3], P('dp'), may hold values from 1 to 8, 12 in all within a row
- attn_weight: bfloat16 [2, 768, 3072], replicated
- attn_bias: bfloat16 [2, 3, 768], replicated, may hold values from -3 to 3
- attn_norm: bfloat16 [2, 2, 768], replicated
- mlp_weight: bfloat16 [2, 2, 768, 3072], replicated
- mlp_bias: bfloat16 [2, 3072], replicated, may hold values from -3 to 3
- mlp_small: bfloat16 [2, 3, 768], replicated
- seg_embed: bfloat16 [8, 768], replicated, may hold values from -3 to 3
- cotangent: bfloat16 [24576, 768], P(('dp', 'section')), may hold values from -6 to 6
Outputs:
- encoded: bfloat16 [24576, 768], P(('dp', 'section'))
- input_grad: bfloat16 [24576, 768], P(('dp', 'section'))
- grad_attn_weight: float32 [2, 768, 3072], P(None, None, ('dp', 'section'))
- grad_attn_bias: float32 [2, 3, 768], replicated
- grad_attn_norm: float32 [2, 2, 768], replicated
- grad_mlp_weight: float32 [2, 2, 768, 3072], P(None, None, None, ('dp', 'section'))
- grad_mlp_bias: float32 [2, 3072], replicated
- grad_mlp_small: float32 [2, 3, 768], replicated
- grad_seg_embed: float32 [8, 768], replicated
Inputs may be any that keep to these rules, and one draw needn't show every extreme that they name: Each row holds the segment counts of the 3 documents of one micro-batch in order; they sum to 12 and one is exactly 8.
All inputs are finite; a program needn't handle non-finite values.
Results may differ from a plain program's by a relative error of at most 0.018.
Values may be sent and summed in bfloat16 or wider, within the bound.
A program may use at most 256 MiB of HBM per device.

v0:
```python
import jax
import jax.numpy as jnp
from jax import lax
from jax.sharding import PartitionSpec as P

HEAD = 64
SEG = 128
MICRO = 2
SEGS = 12
DOCS = 3


HIGHEST = lax.Precision.HIGHEST
masked_score = -1e30


def for_sending(x):
    return jax.tree.map(lambda a: a.astype(jnp.bfloat16) if a.dtype == jnp.float32 else a, x)


def passed_along(value, axis, steps):
    count = lax.axis_size(axis)
    leading, last = (max(0, -steps), min(count, count - steps))
    return lax.ppermute(value, axis, [(source, source + steps) for source in range(leading, last)])


def contract_rows(left, right):
    return lax.dot_general(
        left, right, (((0,), (0,)), ((), ())), preferred_element_type=jnp.float32
    )


def contract_last(left, right):
    return lax.dot_general(
        left, right, (((1,), (1,)), ((), ())), preferred_element_type=jnp.float32
    )


def exact_gelu(values):
    return jax.nn.gelu(values, approximate=False)


def layer_norm(residual, gain_vec, shift_vec):
    center = residual - jnp.mean(residual, axis=-1, keepdims=True)
    spread = jnp.mean(center * center, axis=-1, keepdims=True)
    return center * lax.rsqrt(spread + 1e-05) * gain_vec + shift_vec


def norm_back(residual, gain_vec, shift_vec, grad_out):
    _, pull_back = jax.vjp(layer_norm, residual, gain_vec, shift_vec)
    return pull_back(grad_out)


def doc_layout(seg_counts):
    doc_ends = jnp.cumsum(seg_counts)
    doc_starts = doc_ends - seg_counts
    seg_index = jnp.arange(SEGS, dtype=jnp.int32)
    doc_ids = jnp.sum((seg_index[:, None] >= doc_ends[None, :]).astype(jnp.int32), axis=1)
    doc_index = jnp.arange(DOCS, dtype=jnp.int32)
    own_start = jnp.sum(
        jnp.where(doc_ids[:, None] == doc_index[None, :], doc_starts[None, :], 0), axis=1
    )
    return (doc_ids, seg_index - own_start)


def pick_slot(buffer, slot_idx):
    return lax.dynamic_index_in_dim(buffer, slot_idx, 0, keepdims=False)


def keep_slot(buffer, new_value, slot_idx, active):
    current = pick_slot(buffer, slot_idx)
    return lax.dynamic_update_index_in_dim(
        buffer, jnp.where(active, new_value, current), slot_idx, 0
    )


def attn_core(inputs, weight, offset, length, allowed):
    row_count, model_width = inputs.shape
    head_count = model_width // HEAD
    factor = HEAD ** (-0.5)
    rounded = inputs.astype(jnp.bfloat16)
    zeros_k = jnp.zeros_like(offset[0])
    project = jnp.dot(rounded, weight[:, : 3 * model_width], preferred_element_type=jnp.float32)
    project = project + jnp.concatenate([offset[0], zeros_k, offset[1]]).astype(jnp.float32)
    qkv_all = project.astype(jnp.bfloat16).reshape(row_count // length, length, 3, head_count, HEAD)
    scores = (
        jnp.einsum(
            "gqhd,gkhd->ghqk",
            qkv_all[:, :, 0],
            qkv_all[:, :, 1],
            preferred_element_type=jnp.float32,
        )
        * factor
    )
    scores = jnp.where(allowed, scores, masked_score)
    attn_probs = jax.nn.softmax(scores, axis=-1)
    context = jnp.einsum(
        "ghqk,gkhd->gqhd",
        attn_probs.astype(jnp.bfloat16),
        qkv_all[:, :, 2],
        preferred_element_type=jnp.float32,
    )
    context = context.reshape(row_count, model_width).astype(jnp.bfloat16)
    branch = jnp.dot(
        context, weight[:, 3 * model_width :], preferred_element_type=jnp.float32
    ) + offset[2].astype(jnp.float32)
    return (inputs + branch, (rounded, qkv_all, attn_probs, context))


def attn_back(grad_resid, weight, kept_vals):
    rounded, qkv_all, attn_probs, context = kept_vals
    group_count, length, _, head_count, _ = qkv_all.shape
    model_width = head_count * HEAD
    factor = HEAD ** (-0.5)
    grad_branch = grad_resid.astype(jnp.bfloat16)
    grad_wout = contract_rows(context, grad_branch)
    grad_context = contract_last(grad_branch, weight[:, 3 * model_width :]).astype(jnp.bfloat16)
    grad_context = grad_context.reshape(group_count, length, head_count, HEAD)
    grad_probs = jnp.einsum(
        "gqhd,gkhd->ghqk", grad_context, qkv_all[:, :, 2], preferred_element_type=jnp.float32
    )
    grad_value = jnp.einsum(
        "ghqk,gqhd->gkhd",
        attn_probs.astype(jnp.bfloat16),
        grad_context,
        preferred_element_type=jnp.float32,
    )
    grad_scores = attn_probs * (
        grad_probs - jnp.sum(grad_probs * attn_probs, axis=-1, keepdims=True)
    )
    grad_scores = grad_scores.astype(jnp.bfloat16)
    grad_query = (
        jnp.einsum(
            "ghqk,gkhd->gqhd", grad_scores, qkv_all[:, :, 1], preferred_element_type=jnp.float32
        )
        * factor
    )
    grad_key = (
        jnp.einsum(
            "ghqk,gqhd->gkhd", grad_scores, qkv_all[:, :, 0], preferred_element_type=jnp.float32
        )
        * factor
    )
    grad_qkv = jnp.stack([grad_query, grad_key, grad_value], axis=2)
    grad_qkv = grad_qkv.reshape(group_count * length, 3 * model_width).astype(jnp.bfloat16)
    grad_bias = jnp.stack(
        [
            jnp.sum(grad_qkv[:, :model_width].astype(jnp.float32), axis=0),
            jnp.sum(grad_qkv[:, 2 * model_width :].astype(jnp.float32), axis=0),
            jnp.sum(grad_branch.astype(jnp.float32), axis=0),
        ]
    )
    grad_wqkv = contract_rows(rounded, grad_qkv)
    grad_inputs = grad_resid + contract_last(grad_qkv, weight[:, : 3 * model_width])
    return (grad_inputs, jnp.concatenate([grad_wqkv, grad_wout], axis=1), grad_bias)


def ffn_core(inputs, weight_in, weight_out, offset_in, offset_out):
    hidden = jnp.dot(inputs, weight_in, preferred_element_type=jnp.float32) + offset_in.astype(
        jnp.float32
    )
    active = exact_gelu(hidden).astype(jnp.bfloat16)
    branch = contract_last(active, weight_out) + offset_out.astype(jnp.float32)
    return (inputs.astype(jnp.float32) + branch, (hidden, active))


def ffn_back(grad_resid, inputs, weight_in, weight_out, kept_vals):
    hidden, active = kept_vals
    grad_branch = grad_resid.astype(jnp.bfloat16)
    grad_wout = contract_rows(grad_branch, active)
    grad_active = jnp.dot(grad_branch, weight_out, preferred_element_type=jnp.float32)
    _, gelu_pull = jax.vjp(exact_gelu, hidden)
    grad_hidden = gelu_pull(grad_active)[0].astype(jnp.bfloat16)
    grad_win = contract_rows(inputs, grad_hidden)
    grad_inputs = grad_resid + contract_last(grad_hidden, weight_in)
    offsets = (
        jnp.sum(grad_hidden.astype(jnp.float32), axis=0),
        jnp.sum(grad_branch.astype(jnp.float32), axis=0),
    )
    return (grad_inputs, jnp.stack([grad_win, grad_wout]), offsets)


def on_device(
    tokens,
    counts,
    attn_weight,
    attn_bias,
    attn_norm,
    mlp_weight,
    mlp_bias,
    mlp_small,
    seg_embed,
    cotangent,
):
    section_num = lax.axis_index("section")
    last_section = lax.axis_size("section") - 1
    model_width = tokens.shape[1]
    hidden_width = mlp_bias.shape[1]
    row_span = SEGS * SEG
    norm_attn = attn_norm.astype(jnp.float32)
    norm_mlp = mlp_small.astype(jnp.float32)
    embed_f32 = seg_embed.astype(jnp.float32)

    def leader_inputs(slot_idx, cls_rows):
        doc_ids, seg_pos = doc_layout(pick_slot(counts, slot_idx))
        positions = jnp.arange(seg_embed.shape[0], dtype=jnp.int32)
        onehot = (seg_pos[:, None] == positions[None, :]).astype(jnp.float32)
        leaders = cls_rows.astype(jnp.float32) + jnp.dot(onehot, embed_f32, precision=HIGHEST)
        return (leaders, doc_ids[:, None] == doc_ids[None, :], onehot)

    fed_tokens, fed_cot = (
        lax.all_gather(tokens, "section", axis=0, tiled=True),
        lax.all_gather(cotangent, "section", axis=0, tiled=True),
    )
    fed_tokens = fed_tokens.reshape(MICRO, row_span, model_width)
    fed_cot = fed_cot.reshape(MICRO, row_span, model_width)
    zeros_big = jnp.zeros((row_span, model_width), jnp.bfloat16)
    zeros_small = jnp.zeros((SEGS, model_width), jnp.bfloat16)
    zeros_mat = jnp.zeros((model_width, hidden_width), jnp.float32)
    zeros_vec = jnp.zeros((model_width,), jnp.float32)
    zeros_ff = jnp.zeros((hidden_width,), jnp.float32)
    zeros_table = jnp.zeros(seg_embed.shape, jnp.float32)

    def fwd_first(slot_idx, recv_big, recv_small, skip_in):
        inputs = pick_slot(fed_tokens, slot_idx).astype(jnp.float32)
        residual, _ = attn_core(inputs, attn_weight[0], attn_bias[0], SEG, True)
        return (
            layer_norm(residual, norm_attn[0, 0], norm_attn[0, 1]).astype(jnp.bfloat16),
            zeros_small,
        )

    def fwd_second(slot_idx, recv_big, recv_small, skip_in):
        residual, _ = ffn_core(
            recv_big, mlp_weight[0, 0], mlp_weight[0, 1], mlp_bias[0], mlp_small[0, 0]
        )
        second = layer_norm(residual, norm_mlp[0, 1], norm_mlp[0, 2]).astype(jnp.bfloat16)
        return (second, second.reshape(SEGS, SEG, model_width)[:, 0])

    def fwd_third(slot_idx, recv_big, recv_small, skip_in):
        leaders, allowed, _ = leader_inputs(slot_idx, recv_small)
        residual, _ = attn_core(leaders, attn_weight[1], attn_bias[1], SEGS, allowed)
        third_out = layer_norm(residual, norm_attn[1, 0], norm_attn[1, 1]).astype(jnp.bfloat16)
        return (recv_big, third_out)

    def fwd_fourth(slot_idx, recv_big, recv_small, skip_in):
        residual, _ = ffn_core(
            recv_small, mlp_weight[1, 0], mlp_weight[1, 1], mlp_bias[1], mlp_small[1, 0]
        )
        fourth = layer_norm(residual, norm_mlp[1, 1], norm_mlp[1, 2]).astype(jnp.bfloat16)
        grouped = skip_in.reshape(SEGS, SEG, model_width).at[:, 0].set(fourth)
        return (grouped.reshape(row_span, model_width), zeros_small)

    forward_branches = [fwd_first, fwd_second, fwd_third, fwd_fourth]

    def forward_tick(tick_num, loop_state):
        recv_big, recv_small, skip_now, skip_older, kept_big, kept_small, finals = loop_state
        micro_idx = tick_num - section_num
        active = (micro_idx >= 0) & (micro_idx < MICRO)
        slot_idx = jnp.clip(micro_idx, 0, MICRO - 1)
        skip_in = recv_big
        out_big, out_small = lax.switch(
            section_num, forward_branches, slot_idx, recv_big, recv_small, skip_in
        )
        kept_big = keep_slot(
            kept_big, jnp.where(section_num == last_section, skip_in, recv_big), slot_idx, active
        )
        kept_small = keep_slot(kept_small, recv_small, slot_idx, active)
        finals = keep_slot(finals, out_big, slot_idx, active)
        recv_big, recv_small = (
            passed_along(for_sending(out_big), "section", 1).astype(out_big.dtype),
            passed_along(for_sending(out_small), "section", 1).astype(out_small.dtype),
        )
        return (recv_big, recv_small, skip_now, skip_older, kept_big, kept_small, finals)

    stack_big = jnp.zeros((MICRO, row_span, model_width), jnp.bfloat16)
    stack_small = jnp.zeros((MICRO, SEGS, model_width), jnp.bfloat16)
    start_state = (zeros_big, zeros_small, zeros_big, zeros_big, stack_big, stack_small, stack_big)
    forward_state = lax.fori_loop(0, MICRO + last_section, forward_tick, start_state)
    kept_big, kept_small, finals = (forward_state[4], forward_state[5], forward_state[6])

    def back_first(slot_idx, recv_big, recv_small, skip_in):
        inputs = pick_slot(fed_tokens, slot_idx).astype(jnp.float32)
        residual, kept_vals = attn_core(inputs, attn_weight[0], attn_bias[0], SEG, True)
        grad_resid, grad_gain, grad_shift = norm_back(
            residual, norm_attn[0, 0], norm_attn[0, 1], recv_big.astype(jnp.float32)
        )
        grad_inputs, grad_w, grad_bias = attn_back(grad_resid, attn_weight[0], kept_vals)
        vectors = jnp.concatenate([grad_bias, jnp.stack([grad_gain, grad_shift])])
        return (
            grad_inputs.astype(jnp.bfloat16),
            zeros_small,
            jnp.stack([grad_w, zeros_mat]),
            vectors,
            zeros_ff,
            zeros_table,
        )

    def back_second(slot_idx, recv_big, recv_small, skip_in):
        inputs = pick_slot(kept_big, slot_idx)
        grouped = skip_in.astype(jnp.float32).reshape(SEGS, SEG, model_width)
        grad_out = (
            grouped.at[:, 0].add(recv_small.astype(jnp.float32)).reshape(row_span, model_width)
        )
        residual, kept_vals = ffn_core(
            inputs, mlp_weight[0, 0], mlp_weight[0, 1], mlp_bias[0], mlp_small[0, 0]
        )
        grad_resid, grad_gain, grad_shift = norm_back(
            residual, norm_mlp[0, 1], norm_mlp[0, 2], grad_out
        )
        grad_inputs, grad_mats, offsets = ffn_back(
            grad_resid, inputs, mlp_weight[0, 0], mlp_weight[0, 1], kept_vals
        )
        vectors = jnp.stack([offsets[1], grad_gain, grad_shift, zeros_vec, zeros_vec])
        return (
            grad_inputs.astype(jnp.bfloat16),
            zeros_small,
            grad_mats,
            vectors,
            offsets[0],
            zeros_table,
        )

    def back_third(slot_idx, recv_big, recv_small, skip_in):
        leaders, allowed, onehot = leader_inputs(slot_idx, pick_slot(kept_small, slot_idx))
        residual, kept_vals = attn_core(leaders, attn_weight[1], attn_bias[1], SEGS, allowed)
        grad_resid, grad_gain, grad_shift = norm_back(
            residual, norm_attn[1, 0], norm_attn[1, 1], recv_small.astype(jnp.float32)
        )
        grad_leaders, grad_w, grad_bias = attn_back(grad_resid, attn_weight[1], kept_vals)
        table_part = jnp.dot(onehot.T, grad_leaders, precision=HIGHEST)
        vectors = jnp.concatenate([grad_bias, jnp.stack([grad_gain, grad_shift])])
        return (
            recv_big,
            grad_leaders.astype(jnp.bfloat16),
            jnp.stack([grad_w, zeros_mat]),
            vectors,
            zeros_ff,
            table_part,
        )

    def back_fourth(slot_idx, recv_big, recv_small, skip_in):
        inputs = pick_slot(kept_small, slot_idx)
        cot_rows = pick_slot(fed_cot, slot_idx).reshape(SEGS, SEG, model_width)
        residual, kept_vals = ffn_core(
            inputs, mlp_weight[1, 0], mlp_weight[1, 1], mlp_bias[1], mlp_small[1, 0]
        )
        grad_resid, grad_gain, grad_shift = norm_back(
            residual, norm_mlp[1, 1], norm_mlp[1, 2], cot_rows[:, 0].astype(jnp.float32)
        )
        grad_inputs, grad_mats, offsets = ffn_back(
            grad_resid, inputs, mlp_weight[1, 0], mlp_weight[1, 1], kept_vals
        )
        rest_rows = (
            cot_rows.at[:, 0]
            .set(jnp.zeros((SEGS, model_width), jnp.bfloat16))
            .reshape(row_span, model_width)
        )
        vectors = jnp.stack([offsets[1], grad_gain, grad_shift, zeros_vec, zeros_vec])
        return (
            rest_rows,
            grad_inputs.astype(jnp.bfloat16),
            grad_mats,
            vectors,
            offsets[0],
            zeros_table,
        )

    backward_branches = [back_first, back_second, back_third, back_fourth]

    def backward_tick(tick_num, loop_state):
        recv_big, recv_small, skip_now, skip_older, mats, vectors, ff_grad, table_sum, in_grads = (
            loop_state
        )
        micro_idx = tick_num - (last_section - section_num)
        active = (micro_idx >= 0) & (micro_idx < MICRO)
        slot_idx = jnp.clip(micro_idx, 0, MICRO - 1)
        skip_in = recv_big
        out_big, out_small, grad_mats, grad_vec, grad_ff, grad_table = lax.switch(
            section_num, backward_branches, slot_idx, recv_big, recv_small, skip_in
        )
        mats = mats + jnp.where(active, grad_mats, 0.0)
        vectors = vectors + jnp.where(active, grad_vec, 0.0)
        ff_grad = ff_grad + jnp.where(active, grad_ff, 0.0)
        table_sum = table_sum + jnp.where(active, grad_table, 0.0)
        in_grads = keep_slot(in_grads, out_big, slot_idx, active)
        recv_big, recv_small = (
            passed_along(for_sending(out_big), "section", -1).astype(out_big.dtype),
            passed_along(for_sending(out_small), "section", -1).astype(out_small.dtype),
        )
        return (
            recv_big,
            recv_small,
            skip_now,
            skip_older,
            mats,
            vectors,
            ff_grad,
            table_sum,
            in_grads,
        )

    start_back = (
        zeros_big,
        zeros_small,
        zeros_big,
        zeros_big,
        jnp.zeros((2, model_width, hidden_width), jnp.float32),
        jnp.zeros((5, model_width), jnp.float32),
        zeros_ff,
        zeros_table,
        stack_big,
    )
    back_state = lax.fori_loop(0, MICRO + last_section, backward_tick, start_back)
    mats, vectors, ff_grad, table_grad, in_grads = (
        back_state[4],
        back_state[5],
        back_state[6],
        back_state[7],
        back_state[8],
    )
    out_rows = jnp.where(section_num == last_section, finals.astype(jnp.float32), 0.0).reshape(
        MICRO * row_span, model_width
    )
    grad_rows = jnp.where(section_num == 0, in_grads.astype(jnp.float32), 0.0).reshape(
        MICRO * row_span, model_width
    )
    encoded, input_grad = (
        lax.psum_scatter(
            out_rows.astype(jnp.bfloat16), "section", scatter_dimension=0, tiled=True
        ).astype(jnp.float32),
        lax.psum_scatter(
            grad_rows.astype(jnp.bfloat16), "section", scatter_dimension=0, tiled=True
        ).astype(jnp.float32),
    )
    kind = section_num // 2
    is_attn = section_num % 2 == 0
    reduced = lax.psum_scatter(mats, "dp", scatter_dimension=2, tiled=True)
    placed = lax.all_to_all(
        reduced[None].astype(jnp.bfloat16), "section", split_axis=3, concat_axis=0, tiled=True
    ).astype(jnp.float32)
    grad_attn_weight = jnp.stack([placed[0, 0], placed[2, 0]])
    grad_mlp_weight = jnp.stack([placed[1], placed[3]])
    attn_bias_part = lax.dynamic_update_index_in_dim(
        jnp.zeros((2, 3, model_width), jnp.float32), jnp.where(is_attn, vectors[:3], 0.0), kind, 0
    )
    attn_norm_part = lax.dynamic_update_index_in_dim(
        jnp.zeros((2, 2, model_width), jnp.float32), jnp.where(is_attn, vectors[3:5], 0.0), kind, 0
    )
    mlp_bias_part = lax.dynamic_update_index_in_dim(
        jnp.zeros((2, hidden_width), jnp.float32), jnp.where(is_attn, 0.0, ff_grad), kind, 0
    )
    mlp_small_part = lax.dynamic_update_index_in_dim(
        jnp.zeros((2, 3, model_width), jnp.float32), jnp.where(is_attn, 0.0, vectors[:3]), kind, 0
    )
    grad_attn_bias, grad_attn_norm, grad_mlp_bias, grad_mlp_small, grad_seg_embed = lax.psum(
        (attn_bias_part, attn_norm_part, mlp_bias_part, mlp_small_part, table_grad),
        ("dp", "section"),
    )
    return (
        encoded.astype(jnp.bfloat16),
        input_grad.astype(jnp.bfloat16),
        grad_attn_weight,
        grad_attn_bias,
        grad_attn_norm,
        grad_mlp_weight,
        grad_mlp_bias,
        grad_mlp_small,
        grad_seg_embed,
    )


def solution(mesh):
    return jax.shard_map(
        on_device,
        mesh=mesh,
        in_specs=(
            P(("dp", "section"), None),
            P("dp", None),
            P(),
            P(),
            P(),
            P(),
            P(),
            P(),
            P(),
            P(("dp", "section"), None),
        ),
        out_specs=(
            P(("dp", "section"), None),
            P(("dp", "section"), None),
            P(None, None, ("dp", "section")),
            P(),
            P(),
            P(None, None, None, ("dp", "section")),
            P(),
            P(),
            P(),
        ),
        check_vma=False,
    )
```

profile of v0, /device:TPU:0, one launch (start us, length us, event | category | flops | bytes accessed | tf_op | source)
XLA Modules:
  0.0 3101.9 jit_solution(1278454927214992581)
XLA Ops:
  14.0 35.7 %all-gather.3.cloned.1.call-done = bf16[3072,768]{1,0:T(8,128)(2,1)} async-done(((bf16[768,768]{1,0:T(8,128)(2,1)}), bf16[3072,768]{1,0:T(8,128)(2,1)}) %all-gather.3.cloned.1.call-update) | async-done | bytes 4718608 | tf_op jit(solution)/shard_map/all_gather | solution.py:212
  56.4 32.4 %all-gather.5.cloned.1.call-done = bf16[3072,768]{1,0:T(8,128)(2,1)} async-done(((bf16[768,768]{1,0:T(8,128)(2,1)}), bf16[3072,768]{1,0:T(8,128)(2,1)}) %all-gather.5.cloned.1.call-update) | async-done | bytes 4718608 | tf_op jit(solution)/shard_map/all_gather | solution.py:213
  95.2 749.4 %while.53 = (s32[]{:T(128)}, bf16[1536,768]{1,0:T(8,128)(2,1)S(1)}, bf16[12,768]{1,0:T(8,128)(2,1)}, bf16[2,1536,768]{1,2,0:T(8,128)(2,1)}, bf16[2,12,768]{2,1,0...) while((s32[]{:T(128)}, bf16[1536,768]{1,0:T(8,128)(2,1)S(1)}, ...), condition=%wide.region_20.21_spmd, body=%wide.region_0.20_spmd.sunk | while | flops 14823471104 | bytes 253277456 | solution.py:278
  118.8 108.6 %conditional.5 = (bf16[1536,768]{1,0:T(8,128)(2,1)}, bf16[12,768]{1,0:T(8,128)(2,1)}) conditional(s32[]{:T(128)} %get-tuple-element.2077, (s32[]{:T(128)}, bf16[2,1536,768]{2,1,0:T(8,128)(2,1)}, bf16[2,768,3072]{2,1,0:T(8,128)(2,1)}, bf16[2,3,768]{2,1,0:T(4,128)(2,1)}, f32[2,2,768]{2,1,0:T(2,128)}) %tuple.230, ...), branch_computations={%region_1.5_spmd, %region_6.8_spmd, %region_9.16_spmd, %region_17.... | conditional | flops 14821102592 | bytes 177225360 | solution.py:261
  142.0 21.9 reshape.723
  263.8 108.6 %conditional.5 = (bf16[1536,768]{1,0:T(8,128)(2,1)}, bf16[12,768]{1,0:T(8,128)(2,1)}) conditional(s32[]{:T(128)} %get-tuple-element.2077, (s32[]{:T(128)}, bf16[2,1536,768]{2,1,0:T(8,128)(2,1)}, bf16[2,768,3072]{2,1,0:T(8,128)(2,1)}, bf16[2,3,768]{2,1,0:T(4,128)(2,1)}, f32[2,2,768]{2,1,0:T(2,128)}) %tuple.230, ...), branch_computations={%region_1.5_spmd, %region_6.8_spmd, %region_9.16_spmd, %region_17.... | conditional | flops 14821102592 | bytes 177225360 | solution.py:261
  287.0 21.9 reshape.723
  409.0 108.6 %conditional.5 = (bf16[1536,768]{1,0:T(8,128)(2,1)}, bf16[12,768]{1,0:T(8,128)(2,1)}) conditional(s32[]{:T(128)} %get-tuple-element.2077, (s32[]{:T(128)}, bf16[2,1536,768]{2,1,0:T(8,128)(2,1)}, bf16[2,768,3072]{2,1,0:T(8,128)(2,1)}, bf16[2,3,768]{2,1,0:T(4,128)(2,1)}, f32[2,2,768]{2,1,0:T(2,128)}) %tuple.230, ...), branch_computations={%region_1.5_spmd, %region_6.8_spmd, %region_9.16_spmd, %region_17.... | conditional | flops 14821102592 | bytes 177225360 | solution.py:261
  432.2 21.9 reshape.723
  554.2 108.6 %conditional.5 = (bf16[1536,768]{1,0:T(8,128)(2,1)}, bf16[12,768]{1,0:T(8,128)(2,1)}) conditional(s32[]{:T(128)} %get-tuple-element.2077, (s32[]{:T(128)}, bf16[2,1536,768]{2,1,0:T(8,128)(2,1)}, bf16[2,768,3072]{2,1,0:T(8,128)(2,1)}, bf16[2,3,768]{2,1,0:T(4,128)(2,1)}, f32[2,2,768]{2,1,0:T(2,128)}) %tuple.230, ...), branch_computations={%region_1.5_spmd, %region_6.8_spmd, %region_9.16_spmd, %region_17.... | conditional | flops 14821102592 | bytes 177225360 | solution.py:261
  577.4 21.9 reshape.723
  699.4 108.6 %conditional.5 = (bf16[1536,768]{1,0:T(8,128)(2,1)}, bf16[12,768]{1,0:T(8,128)(2,1)}) conditional(s32[]{:T(128)} %get-tuple-element.2077, (s32[]{:T(128)}, bf16[2,1536,768]{2,1,0:T(8,128)(2,1)}, bf16[2,768,3072]{2,1,0:T(8,128)(2,1)}, bf16[2,3,768]{2,1,0:T(4,128)(2,1)}, f32[2,2,768]{2,1,0:T(2,128)}) %tuple.230, ...), branch_computations={%region_1.5_spmd, %region_6.8_spmd, %region_9.16_spmd, %region_17.... | conditional | flops 14821102592 | bytes 177225360 | solution.py:261
  722.6 21.9 reshape.723
  847.9 1435.0 %while.54 = (s32[]{:T(128)}, bf16[1536,768]{0,1:T(8,128)(2,1)S(1)}, bf16[12,768]{1,0:T(8,128)(2,1)}, f32[2,768,3072]{2,1,0:T(8,128)}, f32[5,768]{1,0:T(8,128)}, ...) while((s32[]{:T(128)}, bf16[1536,768]{0,1:T(8,128)(2,1)S(1)}, ...), condition=%wide.region_70.71_spmd.clone, body=%wide.region_22.70_spmd.clone.sunk | while | flops 43933712384 | bytes 667749440 | solution.py:413
  854.9 257.1 %conditional.6 = (bf16[1536,768]{0,1:T(8,128)(2,1)}, bf16[12,768]{1,0:T(8,128)(2,1)}, f32[2,768,3072]{2,1,0:T(8,128)}, f32[5,768]{1,0:T(8,128)}, f32[3072]{0:T(1024)}, /*index=5*/f32[8,768]{1,0:T(8,128)}) conditional(s32[]{:T(128)} %get-tuple-element.2155, (bf16[1536,768]{0,1:T(8,128)(2,1)S(1)}, ...), branch_computations={%region_23.35_spmd, %region_36.44_spmd, %region_45.60_spmd, %regio... | conditional | flops 43918336000 | bytes 589108352 | solution.py:378
  869.4 21.9 reshape.724
  1131.0 257.1 %conditional.6 = (bf16[1536,768]{0,1:T(8,128)(2,1)}, bf16[12,768]{1,0:T(8,128)(2,1)}, f32[2,768,3072]{2,1,0:T(8,128)}, f32[5,768]{1,0:T(8,128)}, f32[3072]{0:T(1024)}, /*index=5*/f32[8,768]{1,0:T(8,128)}) conditional(s32[]{:T(128)} %get-tuple-element.2155, (bf16[1536,768]{0,1:T(8,128)(2,1)S(1)}, ...), branch_computations={%region_23.35_spmd, %region_36.44_spmd, %region_45.60_spmd, %regio... | conditional | flops 43918336000 | bytes 589108352 | solution.py:378
  1145.5 21.9 reshape.724
  1414.6 257.1 %conditional.6 = (bf16[1536,768]{0,1:T(8,128)(2,1)}, bf16[12,768]{1,0:T(8,128)(2,1)}, f32[2,768,3072]{2,1,0:T(8,128)}, f32[5,768]{1,0:T(8,128)}, f32[3072]{0:T(1024)}, /*index=5*/f32[8,768]{1,0:T(8,128)}) conditional(s32[]{:T(128)} %get-tuple-element.2155, (bf16[1536,768]{0,1:T(8,128)(2,1)S(1)}, ...), branch_computations={%region_23.35_spmd, %region_36.44_spmd, %region_45.60_spmd, %regio... | conditional | flops 43918336000 | bytes 589108352 | solution.py:378
  1429.2 21.9 reshape.724
  1698.2 257.1 %conditional.6 = (bf16[1536,768]{0,1:T(8,128)(2,1)}, bf16[12,768]{1,0:T(8,128)(2,1)}, f32[2,768,3072]{2,1,0:T(8,128)}, f32[5,768]{1,0:T(8,128)}, f32[3072]{0:T(1024)}, /*index=5*/f32[8,768]{1,0:T(8,128)}) conditional(s32[]{:T(128)} %get-tuple-element.2155, (bf16[1536,768]{0,1:T(8,128)(2,1)S(1)}, ...), branch_computations={%region_23.35_spmd, %region_36.44_spmd, %region_45.60_spmd, %regio... | conditional | flops 43918336000 | bytes 589108352 | solution.py:378
  1988.3 257.1 %conditional.6 = (bf16[1536,768]{0,1:T(8,128)(2,1)}, bf16[12,768]{1,0:T(8,128)(2,1)}, f32[2,768,3072]{2,1,0:T(8,128)}, f32[5,768]{1,0:T(8,128)}, f32[3072]{0:T(1024)}, /*index=5*/f32[8,768]{1,0:T(8,128)}) conditional(s32[]{:T(128)} %get-tuple-element.2155, (bf16[1536,768]{0,1:T(8,128)(2,1)S(1)}, ...), branch_computations={%region_23.35_spmd, %region_36.44_spmd, %region_45.60_spmd, %regio... | conditional | flops 43918336000 | bytes 589108352 | solution.py:378
  2311.4 28.2 copy.384
  2339.6 725.8 %all-reduce.8 = bf16[2,768,3072]{1,0,2:T(2,128)(2,1)} all-reduce(f32[2,768,3072]{1,0,2:T(2,128)} %copy.384), channel_id=4, replica_groups=mesh['dp'=8,'section'=4] {'dp'}, use_global_device_ids=true, to_apply=%region_72.73.clone | all-reduce | flops 4718592 | bytes 28311552
  (887 shorter events, 1930.1 us)
Async XLA Ops:
  7.2 42.6 %all-gather.3.cloned.1.call-start = ((), (), s32[]{:S(2)}) async-start(), calls=%async_computation.3 | async-start | bytes 5898240 | tf_op jit(solution)/shard_map/all_gather | solution.py:212
  7.9 80.9 %all-gather.5.cloned.1.call-start = ((), (), s32[]{:S(2)}) async-start(), calls=%async_computation.5 | async-start | bytes 5898240 | tf_op jit(solution)/shard_map/all_gather | solution.py:213
  8.7 3079.8 %all-reduce.7.cloned.1.call-start = ((), (), s32[]{:S(2)}) async-start(), calls=%async_computation.7 | async-start | bytes 196608 | tf_op jit(solution)/shard_map/psum | solution.py:455
  227.4 34.1 %collective-permute-start.1 = (bf16[12,768]{1,0:T(8,128)(2,1)}, bf16[12,768]{1,0:T(8,128)(2,1)S(1)}, u32[]{:S(2)}, u32[]{:S(2)}) collective-permute-start(bf16[12,768]{1,0:T(8,128)(2,1)} %get-tuple-element.1954), channel_id=1, source_target_pairs={{0,1},{1,2},{2,3},{4,5},{5,6},{6,7},{8,9},{9,10},{10,11},{12,13},{... | collective-permute-start | bytes 55304 | tf_op jit(solution)/shard_map/while/body/eval_jaxpr/ppermute | solution.py:24
  228.7 33.4 %collective-permute-start = (bf16[1536,768]{1,0:T(8,128)(2,1)}, bf16[1536,768]{1,0:T(8,128)(2,1)}, u32[]{:S(2)}, u32[]{:S(2)}) collective-permute-start(bf16[1536,768]{1,0:T(8,128)(2,1)} %get-tuple-element.1953), channel_id=1, source_target_pairs={{0,1},{1,2},{2,3},{4,5},{5,6},{6,7},{8,9},{9,10},{10,11},{12,13},{... | collective-permute-start | bytes 7077896 | tf_op jit(solution)/shard_map/while/body/eval_jaxpr/ppermute | solution.py:24
  372.4 34.3 %collective-permute-start.1 = (bf16[12,768]{1,0:T(8,128)(2,1)}, bf16[12,768]{1,0:T(8,128)(2,1)S(1)}, u32[]{:S(2)}, u32[]{:S(2)}) collective-permute-start(bf16[12,768]{1,0:T(8,128)(2,1)} %get-tuple-element.1954), channel_id=1, source_target_pairs={{0,1},{1,2},{2,3},{4,5},{5,6},{6,7},{8,9},{9,10},{10,11},{12,13},{... | collective-permute-start | bytes 55304 | tf_op jit(solution)/shard_map/while/body/eval_jaxpr/ppermute | solution.py:24
  373.7 33.7 %collective-permute-start = (bf16[1536,768]{1,0:T(8,128)(2,1)}, bf16[1536,768]{1,0:T(8,128)(2,1)}, u32[]{:S(2)}, u32[]{:S(2)}) collective-permute-start(bf16[1536,768]{1,0:T(8,128)(2,1)} %get-tuple-element.1953), channel_id=1, source_target_pairs={{0,1},{1,2},{2,3},{4,5},{5,6},{6,7},{8,9},{9,10},{10,11},{12,13},{... | collective-permute-start | bytes 7077896 | tf_op jit(solution)/shard_map/while/body/eval_jaxpr/ppermute | solution.py:24
  517.6 34.3 %collective-permute-start.1 = (bf16[12,768]{1,0:T(8,128)(2,1)}, bf16[12,768]{1,0:T(8,128)(2,1)S(1)}, u32[]{:S(2)}, u32[]{:S(2)}) collective-permute-start(bf16[12,768]{1,0:T(8,128)(2,1)} %get-tuple-element.1954), channel_id=1, source_target_pairs={{0,1},{1,2},{2,3},{4,5},{5,6},{6,7},{8,9},{9,10},{10,11},{12,13},{... | collective-permute-start | bytes 55304 | tf_op jit(solution)/shard_map/while/body/eval_jaxpr/ppermute | solution.py:24
  518.9 33.7 %collective-permute-start = (bf16[1536,768]{1,0:T(8,128)(2,1)}, bf16[1536,768]{1,0:T(8,128)(2,1)}, u32[]{:S(2)}, u32[]{:S(2)}) collective-permute-start(bf16[1536,768]{1,0:T(8,128)(2,1)} %get-tuple-element.1953), channel_id=1, source_target_pairs={{0,1},{1,2},{2,3},{4,5},{5,6},{6,7},{8,9},{9,10},{10,11},{12,13},{... | collective-permute-start | bytes 7077896 | tf_op jit(solution)/shard_map/while/body/eval_jaxpr/ppermute | solution.py:24
  662.8 34.3 %collective-permute-start.1 = (bf16[12,768]{1,0:T(8,128)(2,1)}, bf16[12,768]{1,0:T(8,128)(2,1)S(1)}, u32[]{:S(2)}, u32[]{:S(2)}) collective-permute-start(bf16[12,768]{1,0:T(8,128)(2,1)} %get-tuple-element.1954), channel_id=1, source_target_pairs={{0,1},{1,2},{2,3},{4,5},{5,6},{6,7},{8,9},{9,10},{10,11},{12,13},{... | collective-permute-start | bytes 55304 | tf_op jit(solution)/shard_map/while/body/eval_jaxpr/ppermute | solution.py:24
  664.1 33.7 %collective-permute-start = (bf16[1536,768]{1,0:T(8,128)(2,1)}, bf16[1536,768]{1,0:T(8,128)(2,1)}, u32[]{:S(2)}, u32[]{:S(2)}) collective-permute-start(bf16[1536,768]{1,0:T(8,128)(2,1)} %get-tuple-element.1953), channel_id=1, source_target_pairs={{0,1},{1,2},{2,3},{4,5},{5,6},{6,7},{8,9},{9,10},{10,11},{12,13},{... | collective-permute-start | bytes 7077896 | tf_op jit(solution)/shard_map/while/body/eval_jaxpr/ppermute | solution.py:24
  808.0 34.3 %collective-permute-start.1 = (bf16[12,768]{1,0:T(8,128)(2,1)}, bf16[12,768]{1,0:T(8,128)(2,1)S(1)}, u32[]{:S(2)}, u32[]{:S(2)}) collective-permute-start(bf16[12,768]{1,0:T(8,128)(2,1)} %get-tuple-element.1954), channel_id=1, source_target_pairs={{0,1},{1,2},{2,3},{4,5},{5,6},{6,7},{8,9},{9,10},{10,11},{12,13},{... | collective-permute-start | bytes 55304 | tf_op jit(solution)/shard_map/while/body/eval_jaxpr/ppermute | solution.py:24
  809.3 33.7 %collective-permute-start = (bf16[1536,768]{1,0:T(8,128)(2,1)}, bf16[1536,768]{1,0:T(8,128)(2,1)}, u32[]{:S(2)}, u32[]{:S(2)}) collective-permute-start(bf16[1536,768]{1,0:T(8,128)(2,1)} %get-tuple-element.1953), channel_id=1, source_target_pairs={{0,1},{1,2},{2,3},{4,5},{5,6},{6,7},{8,9},{9,10},{10,11},{12,13},{... | collective-permute-start | bytes 7077896 | tf_op jit(solution)/shard_map/while/body/eval_jaxpr/ppermute | solution.py:24
  1111.9 18.3 collective-permute-start.3
  1388.1 25.8 collective-permute-start.3
  1389.4 24.5 collective-permute-start.2
  1671.7 25.8 collective-permute-start.3
  1673.0 24.5 collective-permute-start.2
  1955.3 32.2 %collective-permute-start.3 = (bf16[12,768]{1,0:T(8,128)(2,1)}, bf16[12,768]{1,0:T(8,128)(2,1)S(1)}, u32[]{:S(2)}, u32[]{:S(2)}) collective-permute-start(bf16[12,768]{1,0:T(8,128)(2,1)} %get-tuple-element.1981), channel_id=1, source_target_pairs={{1,0},{2,1},{3,2},{5,4},{6,5},{7,6},{9,8},{10,9},{11,10},{13,12},{... | collective-permute-start | bytes 55304 | tf_op jit(solution)/shard_map/while/body/eval_jaxpr/ppermute | solution.py:24
  1956.6 30.9 collective-permute-start.2
  2245.4 32.2 %collective-permute-start.3 = (bf16[12,768]{1,0:T(8,128)(2,1)}, bf16[12,768]{1,0:T(8,128)(2,1)S(1)}, u32[]{:S(2)}, u32[]{:S(2)}) collective-permute-start(bf16[12,768]{1,0:T(8,128)(2,1)} %get-tuple-element.1981), channel_id=1, source_target_pairs={{1,0},{2,1},{3,2},{5,4},{6,5},{7,6},{9,8},{10,9},{11,10},{13,12},{... | collective-permute-start | bytes 55304 | tf_op jit(solution)/shard_map/while/body/eval_jaxpr/ppermute | solution.py:24
  2246.7 31.0 collective-permute-start.2
  2285.5 803.0 %reduce-scatter.3.cloned.1.call-start = ((), (), s32[]{:S(2)}) async-start(), calls=%async_computation.4 | async-start | bytes 5898240 | tf_op jit(solution)/shard_map/reduce_scatter | solution.py:428
  2297.5 790.9 %reduce-scatter.5.cloned.1.call-start = ((), (), s32[]{:S(2)}) async-start(), calls=%async_computation.6 | async-start | bytes 5898240 | tf_op jit(solution)/shard_map/reduce_scatter | solution.py:431
  (166 other events, 1338.6 us)
Sparse Core Ops, SparseCore 0:
  9.6 40.1 all-gather.2
  51.3 37.4 all-gather.4
  2285.6 149.4 all-reduce.6
  2438.1 48.9 reduce-scatter.2
  2490.3 47.8 reduce-scatter.4
where the time goes:
time: 3120 us; the launch traced here: 3100 us
  local copies, waits for them, and re-layouts  1230 us (39%)
  blocking collectives  744 us (24%)
  matrix products  473 us (15%)
  other arithmetic  379 us (12%)
  loops' own time  160 us (5%)
  waiting for transfers between devices  69.6 us (2%)
  starting transfers between devices  33.2 us (1%)
    unnamed x1, blocking collectives  726 us
    cond x235, local copies, waits for them, and re-layouts  281 us
    reshape x10, local copies, waits for them, and re-layouts, attn_core(): project.astype(jnp.bfloat16)  219 us
    another operation x5, loops' own time, backward_tick(): lax.switch(section_num, backward_branches, slot_idx, recv_big, recv_small...  122 us
    dynamic_slice x25, local copies, waits for them, and re-layouts, pick_slot(): return lax.dynamic_index_in_dim(buffer, slot_idx, 0, keepdims=False)  97.4 us
    convert_element_type x5, local copies, waits for them, and re-layouts, attn_back(): grad_qkv.reshape(group_count * length, 3 * model_width).astype(jnp.bfloat16)  92.3 us
    dot_general x10, matrix products, attn_core(): jnp.dot(rounded, weight[:, :3 * model_width], preferred_element_type=jnp....  90.4 us
    add x5, other arithmetic, backward_tick(): mats = mats + jnp.where(active, grad_mats, 0.0)  81.4 us
  transfers between devices with their start and end apart: 25, of which 2 were waited for; matrix products, arithmetic and copies ran while one was open for 11% of the time, Pallas kernels for 0%

commit v1 on v0

v1 whole, which is shorter than its diff:
```python
import functools

import jax
import jax.numpy as jnp
from jax import lax
from jax.experimental import pallas as pl
from jax.experimental.pallas import tpu as pltpu
from jax.sharding import PartitionSpec as P

F32 = jnp.float32
BF = jnp.bfloat16
D = 768
FF = 3072
SEG = 128
HEAD = 64
HEADS = 12
PAIRS = 6
MICRO = 2
SEGS = 12
OWN = 6
ROWS = OWN * SEG
BOTH = ("dp", "section")
MASKED = -1e30
VM = pl.BlockSpec(memory_space=pltpu.VMEM)
SM = pl.BlockSpec(memory_space=pltpu.SMEM)
ANY = pl.BlockSpec(memory_space=pl.ANY)


def dot(a, b):
    return jnp.dot(a, b, preferred_element_type=F32)


def dot_nt(a, b):
    return lax.dot_general(a, b, (((1,), (1,)), ((), ())), preferred_element_type=F32)


def dot_tn(a, b):
    return lax.dot_general(a, b, (((0,), (0,)), ((), ())), preferred_element_type=F32)


def gelu_parts(h):
    e = jnp.exp(-0.5 * h * h)
    t = 1.0 / (1.0 + (0.3275911 * 0.7071067811865476) * jnp.abs(h))
    poly = t * (
        0.127414796
        + t * (-0.142248368 + t * (0.7107068705 + t * (-0.7265760135 + t * 0.5307027145)))
    )
    tail = poly * e
    phi = jnp.where(h >= 0.0, 1.0 - tail, tail)
    return h * phi, phi + h * (0.3989422804014327 * e)


def norm_rows(r):
    center = r - jnp.mean(r, axis=-1, keepdims=True)
    rstd = lax.rsqrt(jnp.mean(center * center, axis=-1, keepdims=True) + 1e-5)
    return center * rstd, rstd


def norm_back(dy, n, rstd, gain):
    dyg = dy * gain
    return (
        dyg
        - jnp.mean(dyg, axis=-1, keepdims=True)
        - n * jnp.mean(dyg * n, axis=-1, keepdims=True)
    ) * rstd


def halves(v):
    lane = lax.broadcasted_iota(jnp.int32, v.shape, 1)
    zero = jnp.zeros_like(v)
    return jnp.concatenate([jnp.where(lane < HEAD, v, zero), jnp.where(lane < HEAD, zero, v)], 0)


def unhalve(v):
    top, bottom = v[:SEG], v[SEG:]
    lane = lax.broadcasted_iota(jnp.int32, top.shape, 1)
    return jnp.where(lane < HEAD, top, bottom)


def fold8(v):
    return jnp.sum(v.reshape(v.shape[0] // 8, 8, v.shape[1]), axis=0)


def row(ref, *idx):
    i = idx[-1]
    return ref[idx[:-1] + (slice(i, i + 1), slice(None))].astype(F32)


class Copies:
    def __init__(self, sems):
        self.sems, self.all = sems, []

    def start(self, src, dst):
        copy = pltpu.make_async_copy(src, dst, self.sems.at[len(self.all)])
        copy.start()
        self.all.append(copy)
        return copy


def fwd_kernel(
    x_ref, aw, ab, an, mw, mb, ms,
    second_o, first_o, n1_o, rs1_o, n2_o, rs2_o, qkv_o, p_o, ctx_o, act_o, gp_o, cls_o,
    wq, w1, w2, second, first, n1, rs1, n2, rs2, qkv, p, ctx, act, gp, r, wsem, osem,
):
    outs, loads = Copies(osem), Copies(wsem)
    for j in range(4):
        s = slice(j * D, (j + 1) * D)
        loads.start(aw.at[0, :, s], wq.at[:, s])
    loads.start(mw.at[0, 0], w1)
    loads.start(mw.at[0, 1], w2)
    loads = loads.all
    x = x_ref[...]
    for j in range(3):
        loads[j].wait()
        s = slice(j * D, (j + 1) * D)
        v = dot(x, wq[:, s])
        if j != 1:
            v = v + row(ab, 0, j // 2)
        qkv[:, s] = v.astype(BF)
    outs.start(qkv, qkv_o)

    @pl.loop(0, OWN)
    def _(g):
        rows = pl.ds(pl.multiple_of(g * SEG, SEG), SEG)
        for h in range(PAIRS):
            c = slice(h * 128, (h + 1) * 128)
            q = qkv[rows, c] * jnp.asarray(0.125, BF)
            kc = halves(qkv[rows, D + h * 128 : D + (h + 1) * 128])
            vc = halves(qkv[rows, 2 * D + h * 128 : 2 * D + (h + 1) * 128])
            s = dot_nt(q, kc)
            ps = []
            for i in range(2):
                si = s[:, i * 128 : (i + 1) * 128]
                e = jnp.exp(si - jnp.max(si, axis=-1, keepdims=True))
                ps.append((e / jnp.sum(e, axis=-1, keepdims=True)).astype(BF))
            pp = jnp.concatenate(ps, axis=1)
            p[pl.ds(pl.multiple_of(g * ROWS + h * SEG, SEG), SEG), :] = pp
            ctx[rows, c] = dot(pp, vc).astype(BF)

    outs.start(p, p_o)
    outs.start(ctx, ctx_o)
    loads[3].wait()
    r[...] = x.astype(F32) + dot(ctx[...], wq[:, 3 * D :]) + row(ab, 0, 2)

    @pl.loop(0, ROWS // 64)
    def _(i):
        rows = pl.ds(pl.multiple_of(i * 64, 64), 64)
        n, rs = norm_rows(r[rows, :])
        n1[rows, :] = n.astype(BF)
        rs1[rows, :] = rs
        first[rows, :] = (n * row(an, 0, 0) + row(an, 0, 1)).astype(BF)

    outs.start(n1, n1_o)
    outs.start(rs1, rs1_o)
    outs.start(first, first_o)
    loads[4].wait()
    for j in range(4):
        s = slice(j * D, (j + 1) * D)
        r[...] = dot(first[...], w1[:, s]) + mb[0:1, s].astype(F32)

        @pl.loop(0, ROWS // 32)
        def _(i):
            rows = pl.ds(pl.multiple_of(i * 32, 32), 32)
            a, g = gelu_parts(r[rows, :])
            act[rows, s] = a.astype(BF)
            gp[rows, s] = g.astype(BF)

    outs.start(act, act_o)
    outs.start(gp, gp_o)
    loads[5].wait()
    r[...] = first[...].astype(F32) + dot_nt(act[...], w2[...]) + row(ms, 0, 0)
    cls_o[...] = jnp.zeros_like(cls_o)

    @pl.loop(0, OWN)
    def _(g):
        for part in range(2):
            rows = pl.ds(pl.multiple_of(g * SEG + part * 64, 64), 64)
            n, rs = norm_rows(r[rows, :])
            n2[rows, :] = n.astype(BF)
            rs2[rows, :] = rs
            value = (n * row(ms, 0, 1) + row(ms, 0, 2)).astype(BF)
            second[rows, :] = value
            if part == 0:
                cls_o[pl.ds(g, 1), :] = value[0:1].astype(F32)

    outs.start(n2, n2_o)
    outs.start(rs2, rs2_o)
    outs.start(second, second_o)
    for copy in outs.all:
        copy.wait()


def forward(x, aw, ab, an, mw, mb, ms):
    def big(width, dt=BF):
        return ((ROWS, width), dt)

    specs = [big(D), big(D), big(D), big(1, F32), big(D), big(1, F32), big(3 * D)]
    specs += [((OWN * ROWS, 256), BF), big(D), big(FF), big(FF)]
    shapes = [jax.ShapeDtypeStruct(*s) for s in specs] + [jax.ShapeDtypeStruct((8, D), F32)]
    return pl.pallas_call(
        fwd_kernel,
        out_shape=shapes,
        in_specs=[VM, ANY, VM, VM, ANY, VM, VM],
        out_specs=[ANY] * len(specs) + [VM],
        scratch_shapes=[pltpu.VMEM((D, FF), BF)] * 3
        + [pltpu.VMEM(*s) for s in specs]
        + [
            pltpu.VMEM((ROWS, D), F32),
            pltpu.SemaphoreType.DMA((6,)),
            pltpu.SemaphoreType.DMA((len(specs),)),
        ],
        compiler_params=pltpu.CompilerParams(vmem_limit_bytes=56 * 2**20),
    )(x, aw, ab, an, mw, mb, ms)


def cls_kernel(
    own_ref, other_ref, cown_ref, cother_ref, counts, aw, ab, an, mw, mb, ms, embed,
    fourth_o, dlead_o, cols_o, wide_o, small_o,
    wq, w1, w2, wsem,
):
    loads = Copies(wsem)
    loads.start(aw.at[1], wq)
    loads.start(mw.at[1, 0], w1)
    loads.start(mw.at[1, 1], w2)
    loads = loads.all
    section = lax.axis_index("section")
    per_micro = lax.axis_size("section") // MICRO
    half = lax.rem(section, per_micro)
    micro = section // per_micro
    ends = [counts[micro, 0], counts[micro, 0] + counts[micro, 1]]

    def layout(shape, axis):
        r = lax.broadcasted_iota(jnp.int32, shape, axis)
        seg = jnp.where(r < 8, r, r - 2)
        valid = (r < 6) | ((r >= 8) & (r < 14))
        doc = jnp.where(seg >= ends[0], 1, 0) + jnp.where(seg >= ends[1], 1, 0)
        start = jnp.where(doc == 0, 0, jnp.where(doc == 1, ends[0], ends[1]))
        pos = jnp.where(valid, seg - start, -1)
        return jnp.where(valid, doc, jnp.where(r < 16, 100 + r, -1)), pos, valid

    def order(a_ref, b_ref):
        a, b = a_ref[...], b_ref[...]
        first = half == 0
        return jnp.concatenate([jnp.where(first, a, b), jnp.where(first, b, a)], axis=0)

    def mine(v):
        return jnp.where(half == 0, v[:8], v[8:])

    doc_q, pos, valid = layout((16, 128), 0)
    doc_k, _, _ = layout((16, 128), 1)
    allowed = jnp.concatenate([doc_q == doc_k] * HEADS, axis=0)
    lanes8 = lax.broadcasted_iota(jnp.int32, (16, 8), 1)
    onehot = (pos[:, :8] == lanes8).astype(BF)
    leaders = order(own_ref, other_ref) + dot(onehot, embed[...])
    low = leaders.astype(BF)
    lane = lax.broadcasted_iota(jnp.int32, (16, D), 1) // HEAD

    def stack(v):
        return jnp.concatenate([jnp.where(lane == h, v, jnp.zeros_like(v)) for h in range(HEADS)], 0)

    def unstack(v):
        total = jnp.where(lane == 0, v[:16], 0.0)
        for h in range(1, HEADS):
            total = total + jnp.where(lane == h, v[h * 16 : (h + 1) * 16], 0.0)
        return total

    def deep(v):
        return jnp.concatenate([v, jnp.zeros((112, D), BF)], axis=0)

    loads[0].wait()
    q = (dot(low, wq[:, :D]) + row(ab, 1, 0)).astype(BF)
    k = dot(low, wq[:, D : 2 * D]).astype(BF)
    v = (dot(low, wq[:, 2 * D : 3 * D]) + row(ab, 1, 1)).astype(BF)
    qs, kd, vd = stack(q), deep(k), deep(v)
    scores = jnp.where(allowed, dot_nt(qs, kd) * 0.125, MASKED)
    e = jnp.exp(scores - jnp.max(scores, axis=-1, keepdims=True))
    probs = e / jnp.sum(e, axis=-1, keepdims=True)
    probs_low = probs.astype(BF)
    ctx = unstack(dot(probs_low, vd)).astype(BF)
    n1, rs1 = norm_rows(leaders + dot(ctx, wq[:, 3 * D :]) + row(ab, 1, 2))
    third = (n1 * row(an, 1, 0) + row(an, 1, 1)).astype(BF)
    loads[1].wait()
    act, gp = gelu_parts(dot(third, w1[...]) + mb[1:2, :].astype(F32))
    act = act.astype(BF)
    loads[2].wait()
    n2, rs2 = norm_rows(third.astype(F32) + dot_nt(act, w2[...]) + row(ms, 1, 0))
    fourth_o[...] = mine(n2 * row(ms, 1, 1) + row(ms, 1, 2))

    dy = order(cown_ref, cother_ref)
    small_o[10:11, :] = jnp.sum(mine(dy * n2), axis=0, keepdims=True)
    small_o[11:12, :] = jnp.sum(mine(dy), axis=0, keepdims=True)
    dr = norm_back(dy, n2, rs2, row(ms, 1, 1))
    dbf = dr.astype(BF)
    small_o[9:10, :] = jnp.sum(mine(dbf.astype(F32)), axis=0, keepdims=True)
    dh = (dot(dbf, w2[...]) * gp).astype(BF)
    dh_mine = mine(dh.astype(F32))
    dh_sum = jnp.sum(dh_mine, axis=0, keepdims=True)
    for j in range(4):
        small_o[5 + j : 6 + j, :] = dh_sum[:, j * D : (j + 1) * D]
    dthird = (dr + dot_nt(dh, w1[...])).astype(BF).astype(F32)
    small_o[3:4, :] = jnp.sum(mine(dthird * n1), axis=0, keepdims=True)
    small_o[4:5, :] = jnp.sum(mine(dthird), axis=0, keepdims=True)
    dr = norm_back(dthird, n1, rs1, row(an, 1, 0))
    dba = dr.astype(BF)
    small_o[2:3, :] = jnp.sum(mine(dba.astype(F32)), axis=0, keepdims=True)
    dctx = stack(dot_nt(dba, wq[:, 3 * D :]).astype(BF))
    dp = dot_nt(dctx, vd)
    dv = dot_tn(probs_low, dctx)[:16].astype(BF)
    ds = (probs * (dp - jnp.sum(dp * probs, axis=-1, keepdims=True))).astype(BF)
    dq = (unstack(dot(ds, kd)) * 0.125).astype(BF)
    dk = (dot_tn(ds, qs)[:16] * 0.125).astype(BF)
    small_o[0:1, :] = jnp.sum(mine(dq.astype(F32)), axis=0, keepdims=True)
    small_o[1:2, :] = jnp.sum(mine(dv.astype(F32)), axis=0, keepdims=True)
    dlead = dr + dot_nt(dq, wq[:, :D]) + dot_nt(dk, wq[:, D : 2 * D])
    dlead = dlead + dot_nt(dv, wq[:, 2 * D : 3 * D])
    dlead_mine = mine(dlead)
    dlead_o[...] = dlead_mine
    pos_mine = jnp.where(half == 0, pos[:8], pos[8:])
    for i in range(8):
        hit = jnp.where(pos_mine[:, 0:1] == i, dlead_mine, 0.0)
        small_o[12 + i : 13 + i, :] = jnp.sum(hit, axis=0, keepdims=True)
    for j, piece in enumerate((dq, dk, dv, dba)):
        cols_o[0, :, j * D : (j + 1) * D] = mine(piece.astype(F32)).astype(BF)
    cols_o[1] = dh_mine.astype(BF)
    cols_o[2] = mine(act.astype(F32)).astype(BF)
    for j, piece in enumerate((low, ctx, third, dbf)):
        wide_o[j] = mine(piece.astype(F32)).astype(BF)


def cls_chain(own, other, cown, cother, counts, aw, ab, an, mw, mb, ms, embed):
    shapes = [((8, D), F32), ((8, D), F32), ((3, 8, FF), BF), ((4, 8, D), BF), ((20, D), F32)]
    return pl.pallas_call(
        cls_kernel,
        out_shape=[jax.ShapeDtypeStruct(*s) for s in shapes],
        in_specs=[VM, VM, VM, VM, SM, ANY, VM, VM, ANY, VM, VM, VM],
        out_specs=[VM] * 5,
        scratch_shapes=[pltpu.VMEM((D, FF), BF)] * 3 + [pltpu.SemaphoreType.DMA((3,))],
        compiler_params=pltpu.CompilerParams(vmem_limit_bytes=56 * 2**20),
    )(own, other, cown, cother, counts, aw, ab, an, mw, mb, ms, embed)


def bwd_kernel(
    cot, dlead, x, n1_i, rs1_i, n2_i, rs2_i, first_i, qkv_i, p_i, ctx_i, act_i, gp_i,
    aw, an, mw, ms,
    dx_o, dw_o, small_o,
    wq, w1, w2, first, n1, rs1, n2, rs2, qkv, p, ctx, act, gp,
    r, db, dqkv, dctx, dw, sums, wsem, osem,
):
    loads = Copies(wsem)
    for src, dst in (
        (n2_i, n2), (rs2_i, rs2), (act_i, act), (mw.at[0, 1], w2), (gp_i, gp), (first_i, first),
        (mw.at[0, 0], w1), (n1_i, n1), (rs1_i, rs1), (ctx_i, ctx), (aw.at[0], wq), (qkv_i, qkv), (p_i, p),
    ):
        loads.start(src, dst)
    loads = loads.all
    pending = [None, None]
    count = [0]

    def put(value, which, start):
        slot = count[0] % 2
        if pending[slot] is not None:
            pending[slot].wait()
        dw[slot] = value.astype(BF)
        copy = pltpu.make_async_copy(dw.at[slot], dw_o.at[which, start : start + D, :], osem.at[slot])
        copy.start()
        pending[slot] = copy
        count[0] += 1

    sums[...] = jnp.zeros_like(sums)

    def norm_step(rows, dy, n_ref, rs_ref, gain, at):
        n = n_ref[rows, :].astype(F32)
        dr = norm_back(dy, n, rs_ref[rows, :], gain)
        r[rows, :] = dr
        low = dr.astype(BF)
        db[rows, :] = low
        sums[at] += fold8(low.astype(F32))
        sums[at + 1] += fold8(dy * n)
        sums[at + 2] += fold8(dy)

    loads[0].wait()
    loads[1].wait()

    @pl.loop(0, OWN)
    def _(g):
        for part in range(2):
            rows = pl.ds(pl.multiple_of(g * SEG + part * 64, 64), 64)
            dy = cot[rows, :].astype(F32)
            if part == 0:
                cls = lax.broadcasted_iota(jnp.int32, (64, D), 0) == 0
                lead = dlead[pl.ds(g, 1), :].astype(BF).astype(F32)
                dy = jnp.where(cls, lead, dy)
            norm_step(rows, dy, n2, rs2, row(ms, 0, 1), 0)

    loads[2].wait()
    for j in range(4):
        put(dot_tn(act[:, j * D : (j + 1) * D], db[...]), 2, j * D)
    loads[3].wait()
    loads[4].wait()
    for j in range(4):
        s = slice(j * D, (j + 1) * D)
        low = (dot(db[...], w2[:, s]) * gp[:, s].astype(F32)).astype(BF)
        gp[:, s] = low
        sums[6 + j] = fold8(low.astype(F32))
    loads[5].wait()
    for j in range(4):
        put(dot_tn(gp[:, j * D : (j + 1) * D], first[...]), 1, j * D)
    loads[6].wait()
    r[...] += dot_nt(gp[...], w1[...])
    loads[7].wait()
    loads[8].wait()

    @pl.loop(0, ROWS // 64)
    def _(i):
        rows = pl.ds(pl.multiple_of(i * 64, 64), 64)
        dy = r[rows, :].astype(BF).astype(F32)
        norm_step(rows, dy, n1, rs1, row(an, 0, 0), 3)

    loads[9].wait()
    put(dot_tn(db[...], ctx[...]), 0, 3 * D)
    loads[10].wait()
    dctx[...] = dot_nt(db[...], wq[:, 3 * D :]).astype(BF)
    loads[11].wait()
    loads[12].wait()

    @pl.loop(0, OWN)
    def _(g):
        rows = pl.ds(pl.multiple_of(g * SEG, SEG), SEG)
        for h in range(PAIRS):
            cq = slice(h * 128, (h + 1) * 128)
            ck = slice(D + h * 128, D + (h + 1) * 128)
            cv = slice(2 * D + h * 128, 2 * D + (h + 1) * 128)
            q = qkv[rows, cq]
            kc, vc = halves(qkv[rows, ck]), halves(qkv[rows, cv])
            dc = dctx[rows, cq]
            pp = p[pl.ds(pl.multiple_of(g * ROWS + h * SEG, SEG), SEG), :]
            dp = dot_nt(dc, vc)
            pf = pp.astype(F32)
            ds = []
            for i in range(2):
                c = slice(i * 128, (i + 1) * 128)
                pi, di = pf[:, c], dp[:, c]
                ds.append((pi * (di - jnp.sum(di * pi, axis=-1, keepdims=True))).astype(BF))
            ds = jnp.concatenate(ds, axis=1)
            dqkv[rows, cq] = (dot(ds, kc) * 0.125).astype(BF)
            dqkv[rows, ck] = (unhalve(dot_tn(ds, q)) * 0.125).astype(BF)
            dqkv[rows, cv] = unhalve(dot_tn(pp, dc)).astype(BF)

    for j in range(3):
        s = slice(j * D, (j + 1) * D)
        put(dot_tn(dqkv[:, s], x[...]), 0, j * D)
        if j != 1:
            sums[10 + j // 2] = fold8(dqkv[:, s].astype(F32))
    dx_o[...] = (r[...] + dot_nt(dqkv[...], wq[:, : 3 * D])).astype(BF)
    for i, at in enumerate((10, 11, 3, 4, 5, 6, 7, 8, 9, 0, 1, 2)):
        small_o[i : i + 1, :] = jnp.sum(sums[at], axis=0, keepdims=True)
    for copy in pending:
        copy.wait()


def backward(cot, dlead, x, n1, rs1, n2, rs2, first, qkv, p, ctx, act, gp, aw, an, mw, ms):
    shapes = [((ROWS, D), BF), ((3, FF, D), BF), ((12, D), F32)]
    kept = (first, n1, rs1, n2, rs2, qkv, p, ctx, act, gp)
    return pl.pallas_call(
        bwd_kernel,
        out_shape=[jax.ShapeDtypeStruct(*s) for s in shapes],
        in_specs=[VM, VM, VM] + [ANY] * 11 + [VM, ANY, VM],
        out_specs=[VM, ANY, VM],
        scratch_shapes=[pltpu.VMEM((D, FF), BF)] * 3
        + [pltpu.VMEM(a.shape, a.dtype) for a in kept]
        + [
            pltpu.VMEM((ROWS, D), F32),
            pltpu.VMEM((ROWS, D), BF),
            pltpu.VMEM((ROWS, 3 * D), BF),
            pltpu.VMEM((ROWS, D), BF),
            pltpu.VMEM((2, D, D), BF),
            pltpu.VMEM((12, 8, D), F32),
            pltpu.SemaphoreType.DMA((13,)),
            pltpu.SemaphoreType.DMA((2,)),
        ],
        compiler_params=pltpu.CompilerParams(vmem_limit_bytes=60 * 2**20),
    )(cot, dlead, x, n1, rs1, n2, rs2, first, qkv, p, ctx, act, gp, aw, an, mw, ms)


def place_kernel(red, cols, wide, ga_o, gm_o):
    width = red.shape[1]
    me = lax.axis_index("dp") * lax.axis_size("section") + lax.axis_index("section")
    right = jnp.where(me * width >= 3 * D, wide[1].astype(F32), wide[0].astype(F32)).astype(BF)
    ga_o[0] = red[0].astype(F32).T
    gm_o[0, 0] = red[1].astype(F32).T
    gm_o[0, 1] = red[2].astype(F32).T
    ga_o[1] = dot_tn(right, cols[0])
    gm_o[1, 0] = dot_tn(wide[2], cols[1])
    gm_o[1, 1] = dot_tn(wide[3], cols[2])


def place(red, cols, wide):
    width = red.shape[1]
    return pl.pallas_call(
        place_kernel,
        out_shape=[
            jax.ShapeDtypeStruct((2, D, width), F32),
            jax.ShapeDtypeStruct((2, 2, D, width), F32),
        ],
        in_specs=[VM] * 3,
        out_specs=[VM] * 2,
        compiler_params=pltpu.CompilerParams(vmem_limit_bytes=56 * 2**20),
    )(red, cols, wide)


def swap_half(v):
    size = lax.axis_size("section")
    per_micro = size // MICRO
    return lax.ppermute(v, "section", [(i, i - i % per_micro + (i + 1) % per_micro) for i in range(size)])


def on_device(tokens, counts, aw, ab, an, mw, mb, ms, embed, cot):
    cls_cot = jnp.pad(cot.reshape(OWN, SEG, D)[:, 0].astype(F32), ((0, 2), (0, 0)))
    cls_cot_other = swap_half(cls_cot)
    second, first, n1, rs1, n2, rs2, qkv, p, ctx, act, gp, cls = forward(tokens, aw, ab, an, mw, mb, ms)
    fourth, dlead, cols, wide, small1 = cls_chain(
        cls, swap_half(cls), cls_cot, cls_cot_other, counts, aw, ab, an, mw, mb, ms, embed
    )
    cols = lax.all_to_all(cols, BOTH, split_axis=2, concat_axis=1, tiled=True)
    wide = lax.all_gather(wide, BOTH, axis=1, tiled=True)
    encoded = second.reshape(OWN, SEG, D).at[:, 0].set(fourth[:OWN].astype(BF)).reshape(ROWS, D)
    dx, dw, small0 = backward(
        cot, dlead, tokens, n1, rs1, n2, rs2, first, qkv, p, ctx, act, gp, aw, an, mw, ms
    )
    red = lax.psum_scatter(dw, BOTH, scatter_dimension=1, tiled=True)
    small = lax.psum(jnp.concatenate([small0, small1], axis=0), BOTH)
    ga, gm = place(red, cols, wide)
    return (
        encoded,
        dx,
        ga,
        jnp.stack([small[0:3], small[12:15]]),
        jnp.stack([small[3:5], small[15:17]]),
        gm,
        jnp.stack([small[5:9].reshape(FF), small[17:21].reshape(FF)]),
        jnp.stack([small[9:12], small[21:24]]),
        small[24:32],
    )


def solution(mesh):
    return jax.shard_map(
        on_device,
        mesh=mesh,
        in_specs=(P(BOTH, None), P("dp", None)) + (P(),) * 7 + (P(BOTH, None),),
        out_specs=(
            P(BOTH, None),
            P(BOTH, None),
            P(None, None, BOTH),
            P(),
            P(),
            P(None, None, None, BOTH),
            P(),
            P(),
            P(),
        ),
        check_vma=False,
    )
```

time: 3120 us -> 489 us (0.16)
  local copies, waits for them, and re-layouts: 1230 us -> 29.7 us
  blocking collectives: 744 us -> 0 us
  matrix products: 473 us -> 0 us
  other arithmetic: 379 us -> 2.71 us
  waiting for transfers between devices: 69.6 us -> 321 us
  loops' own time: 160 us -> 0 us
  Pallas kernels: 0 us -> 110 us
    unnamed x1 -> x0, blocking collectives: 726 us -> none
    dot_general x80 -> x0, matrix products: 473 us -> none  [the longest x10 90.4 us: attn_core(): jnp.dot(rounded, weight[:, :3 * model_width], preferred_element_type=jnp....]
    reshape x30 -> x0, local copies, waits for them, and re-layouts: 296 us -> none  [the longest x10 219 us: attn_core(): project.astype(jnp.bfloat16)]
    cond x235 -> x0, local copies, waits for them, and re-layouts: 281 us -> none
    reduce_scatter x2 -> x1, waiting for transfers between devices: 0.01 us -> 168 us  [on_device(): red = lax.psum_scatter(dw, BOTH, scatter_dimension=1, tiled=True)]
    another operation x12 -> x0, loops' own time: 160 us -> none  [the longest x5 122 us: backward_tick(): lax.switch(section_num, backward_branches, slot_idx, recv_big, recv_small...]
    slice x21 -> x2, local copies, waits for them, and re-layouts: 150 us -> 2.24 us  [the longest x1 1.35 us: on_device(): small[24:32]]
    convert_element_type x18 -> x0, local copies, waits for them, and re-layouts: 126 us -> none  [the longest x5 92.3 us: attn_back(): grad_qkv.reshape(group_count * length, 3 * model_width).astype(jnp.bfloat16)]
  transfers between devices with their start and end apart: 25 -> 6, of which waited for: 2 -> 4; matrix products, arithmetic and copies ran while one was open for 11% -> 5% of each run, Pallas kernels for 0% -> 0%
where the time goes in v1:
time: 489 us; the launch traced here: 485 us
  waiting for transfers between devices  321 us (66%)
  Pallas kernels  110 us (22%)
  local copies, waits for them, and re-layouts  29.7 us (6%)
  between operations  14.1 us (3%)
  starting transfers between devices  7.77 us (2%)
    reduce_scatter x1, waiting for transfers between devices, on_device(): red = lax.psum_scatter(dw, BOTH, scatter_dimension=1, tiled=True)  168 us
    psum x1, waiting for transfers between devices, on_device(): small = lax.psum(jnp.concatenate([small0, small1], axis=0), BOTH)  106 us
    pallas_call x1, Pallas kernels, backward(): pl.pallas_call(bwd_kernel, out_shape=[jax.ShapeDtypeStruct(*s) for s in s...  54 us
    all_gather x1, waiting for transfers between devices, on_device(): wide = lax.all_gather(wide, BOTH, axis=1, tiled=True)  43.5 us
    pallas_call x1, Pallas kernels, forward(): pl.pallas_call(fwd_kernel, out_shape=shapes, in_specs=[VM, ANY, VM, VM, A...  39.8 us
    unnamed x24, local copies, waits for them, and re-layouts  16.8 us
    pallas_call x1, Pallas kernels, cls_chain(): pl.pallas_call(cls_kernel, out_shape=[jax.ShapeDtypeStruct(*s) for s in s...  13 us
  transfers between devices with their start and end apart: 6, of which 4 were waited for; matrix products, arithmetic and copies ran while one was open for 5% of the time, Pallas kernels for 0%

profile of v1, /device:TPU:0, one launch (start us, length us, event | category | flops | bytes accessed | tf_op | source)
XLA Modules:
  0.0 485.2 jit_solution(3524165734036475156)
XLA Ops:
  7.2 1.3 copy.42.ab
  8.5 1.3 copy.43.ms
  9.8 39.8 %shard_map.169 = (bf16[768,768]{1,0:T(8,128)(2,1)}, bf16[768,768]{1,0:T(8,128)(2,1)}, bf16[768,768]{1,0:T(8,128)(2,1)}, f32[768,1]{1,0:T(8,128)}, bf16[768,768]{...) custom-call(bf16[768,768]{1,0:T(8,128)(2,1)} %x.3, ...), custom_call_target="tpu_custom_call" | custom-call | tf_op jit(solution)/shard_map/pallas_call | solution.py:200
  50.1 0.9 slice.65
  51.2 1.1 collective-permute-done.1.cother_ref
  52.9 13.0 %shard_map.170 = (f32[8,768]{1,0:T(8,128)}, f32[8,768]{1,0:T(8,128)}, bf16[3,8,3072]{2,1,0:T(8,128)(2,1)}, bf16[4,8,768]{2,1,0:T(8,128)(2,1)}, f32[20,768]{1,0:T(8,128)}) custom-call(f32[8,768]{1,0:T(8,128)} %get-tuple-element.44.own_ref, f32[8,768]{1,0:T(8,128)} %copy-done.3, f32[8,768]{1,0:T(8,128)} %copy-done.1, f32[8,768]{1,0:T(8,128)} %copy-done.4, ...), custom_call_target="tpu_custom_call" | custom-call | tf_op jit(solution)/shard_map/pallas_call | solution.py:332
  65.9 54.0 %shard_map.171 = (bf16[768,768]{1,0:T(8,128)(2,1)}, bf16[3,3072,768]{2,1,0:T(8,128)(2,1)}, f32[12,768]{1,0:T(8,128)}) custom-call(bf16[768,768]{1,0:T(8,128)(2,1)} %cot.1, f32[8,768]{1,0:T(8,128)} %get-tuple-element.46.dlead, bf16[768,768]{1,0:T(8,128)(2,1)} %x.3, bf16[768,768]{1,0:T(8,128)(2,1)} %get-tuple-element.47.n1_i, ...), custom_call_target="tpu_custom_call" | custom-call | tf_op jit(solution)/shard_map/pallas_call | solution.py:464
  119.9 1.5 pad_maximum_fusion
  123.1 3.4 copy.49
  126.5 3.4 reshape.66
  129.9 7.0 %all-to-all-start = ((bf16[32,2,1152]{2,1,0:T(2,128)(2,1)}), bf16[32,2,1152]{2,1,0:T(2,128)(2,1)S(1)}, u32[]{:S(2)}, u32[]{:S(2)}) async-start(bf16[32,2,1152]{2,1,0:T(2,128)(2,1)} %reshape.66), calls=%async_computation.1 | async-start | bytes 294912 | tf_op jit(solution)/shard_map/all_to_all | solution.py:524
  136.9 1.6 scatter.4
  138.5 106.2 %all-reduce.3.cloned.1.call-done = f32[32,768]{1,0:T(8,128)} async-done(((f32[32,768]{1,0:T(8,128)}), f32[32,768]{1,0:T(8,128)}) %all-reduce.3.cloned.1.call-update) | async-done | bytes 98320 | tf_op jit(solution)/shard_map/psum | solution.py:531
  244.7 0.8 slice_bitcast_fusion.1
  246.2 0.8 slice_bitcast_fusion.3
  247.6 1.3 slice.75
  249.0 0.8 slice_bitcast_fusion.7
  251.0 2.8 reshape.67
  253.9 4.1 copy.50
  258.0 43.5 %all-gather.2.cloned.1.call-done.wide = bf16[4,256,768]{2,1,0:T(8,128)(2,1)} async-done(((bf16[4,8,768]{2,1,0:T(8,128)(2,1)}), bf16[4,256,768]{2,1,0:T(8,128)(2,1)}) %all-gather.2.cloned.1.call-update) | async-done | bytes 1572880 | tf_op jit(solution)/shard_map/all_gather | solution.py:525
  301.4 168.4 %reduce-scatter.2.cloned.1.call-done.red = bf16[3,96,768]{2,1,0:T(8,128)(2,1)} async-done(((bf16[3,3072,768]{2,1,0:T(8,128)(2,1)}), bf16[3,96,768]{2,1,0:T(8,128)(2,1)}) %reduce-scatter.2.cloned.1.call-update) | async-done | bytes 442384 | tf_op jit(solution)/shard_map/reduce_scatter | solution.py:530
  469.9 3.5 shard_map.172
  473.4 2.2 copy.51
  475.6 2.9 copy.53
  (33 shorter events, 5.5 us)
Async XLA Ops:
  7.2 237.5 %all-reduce.3.cloned.1.call-start = ((), (), s32[]{:S(2)}) async-start(), calls=%async_computation.4 | async-start | bytes 196608 | tf_op jit(solution)/shard_map/psum | solution.py:531
  49.6 1.6 collective-permute-start
  51.1 1.3 copy-start.1
  51.1 1.3 collective-permute-start.1
  51.2 1.1 copy-start.3
  52.3 0.6 copy-start.4
  65.9 54.0 %copy-start.2 = (f32[20,768]{1,0:T(8,128)S(1)}, f32[20,768]{1,0:T(8,128)}, u32[]{:S(2)}) copy-start(f32[20,768]{1,0:T(8,128)} %get-tuple-element.63) | copy-start | bytes 184324
  121.4 180.0 %all-gather.2.cloned.1.call-start = ((), (), s32[]{:S(2)}) async-start(), calls=%async_computation.3 | async-start | bytes 1622016 | tf_op jit(solution)/shard_map/all_gather | solution.py:525
  122.2 347.7 %reduce-scatter.2.cloned.1.call-start = ((), (), s32[]{:S(2)}) async-start(), calls=%async_computation.2 | async-start | bytes 14598144 | tf_op jit(solution)/shard_map/reduce_scatter | solution.py:530
  122.2 0.7 copy-start.5
  122.2 0.9 copy-start
  129.9 121.1 %all-to-all-start = ((bf16[32,2,1152]{2,1,0:T(2,128)(2,1)}), bf16[32,2,1152]{2,1,0:T(2,128)(2,1)S(1)}, u32[]{:S(2)}, u32[]{:S(2)}) async-start(bf16[32,2,1152]{2,1,0:T(2,128)(2,1)} %reshape.66), calls=%async_computation.1 | async-start | bytes 294912 | tf_op jit(solution)/shard_map/all_to_all | solution.py:524
Sparse Core Ops, SparseCore 0:
  121.5 123.0 all-reduce.2
  247.6 53.8 all-gather.1
  307.4 162.3 reduce-scatter.1

commit v2 on v1

--- a/solution.py
+++ b/solution.py
@@ -24,6 +24,7 @@
 VM = pl.BlockSpec(memory_space=pltpu.VMEM)
 SM = pl.BlockSpec(memory_space=pltpu.SMEM)
 ANY = pl.BlockSpec(memory_space=pl.ANY)
+MESH = pl.DeviceIdType.MESH
 
 
 def dot(a, b):
@@ -319,16 +320,21 @@
     for i in range(8):
         hit = jnp.where(pos_mine[:, 0:1] == i, dlead_mine, 0.0)
         small_o[12 + i : 13 + i, :] = jnp.sum(hit, axis=0, keepdims=True)
-    for j, piece in enumerate((dq, dk, dv, dba)):
-        cols_o[0, :, j * D : (j + 1) * D] = mine(piece.astype(F32)).astype(BF)
-    cols_o[1] = dh_mine.astype(BF)
-    cols_o[2] = mine(act.astype(F32)).astype(BF)
-    for j, piece in enumerate((low, ctx, third, dbf)):
-        wide_o[j] = mine(piece.astype(F32)).astype(BF)
+    zeros = jnp.zeros((8, D), F32)
+
+    def pack(top, bottom):
+        return jnp.concatenate([top, bottom], axis=0).astype(BF)
+
+    cols_o[0] = pack(dh_mine, mine(act.astype(F32)))
+    for j, piece in enumerate((dq, dk, dv)):
+        cols_o[1, :, j * D : (j + 1) * D] = pack(mine(piece.astype(F32)), zeros)
+    cols_o[1, :, 3 * D :] = pack(zeros, mine(dba.astype(F32)))
+    wide_o[0] = pack(mine(third.astype(F32)), mine(dbf.astype(F32)))
+    wide_o[1] = pack(mine(low.astype(F32)), mine(ctx.astype(F32)))
 
 
 def cls_chain(own, other, cown, cother, counts, aw, ab, an, mw, mb, ms, embed):
-    shapes = [((8, D), F32), ((8, D), F32), ((3, 8, FF), BF), ((4, 8, D), BF), ((20, D), F32)]
+    shapes = [((8, D), F32), ((8, D), F32), ((2, 16, FF), BF), ((2, 16, D), BF), ((20, D), F32)]
     return pl.pallas_call(
         cls_kernel,
         out_shape=[jax.ShapeDtypeStruct(*s) for s in shapes],
@@ -482,16 +488,20 @@
     )(cot, dlead, x, n1, rs1, n2, rs2, first, qkv, p, ctx, act, gp, aw, an, mw, ms)
 
 
+def cls_grads(wide, cols, ga_o, gm_o, pick):
+    w0, c0 = wide[0], cols[0]
+    low = lax.rem(lax.broadcasted_iota(jnp.int32, c0.shape, 0), 16) < 8
+    zero = jnp.zeros_like(c0)
+    gm_o[1, 0] = dot_tn(w0, pick(jnp.where(low, c0, zero)))
+    gm_o[1, 1] = dot_tn(w0, pick(jnp.where(low, zero, c0)))
+    ga_o[1] = dot_tn(wide[1], pick(cols[1]))
+
+
 def place_kernel(red, cols, wide, ga_o, gm_o):
-    width = red.shape[1]
-    me = lax.axis_index("dp") * lax.axis_size("section") + lax.axis_index("section")
-    right = jnp.where(me * width >= 3 * D, wide[1].astype(F32), wide[0].astype(F32)).astype(BF)
     ga_o[0] = red[0].astype(F32).T
     gm_o[0, 0] = red[1].astype(F32).T
     gm_o[0, 1] = red[2].astype(F32).T
-    ga_o[1] = dot_tn(right, cols[0])
-    gm_o[1, 0] = dot_tn(wide[2], cols[1])
-    gm_o[1, 1] = dot_tn(wide[3], cols[2])
+    cls_grads(wide, cols, ga_o, gm_o, lambda v: v)
 
 
 def place(red, cols, wide):
@@ -508,6 +518,366 @@
     )(red, cols, wide)
 
 
+class Place:
+    def __init__(self):
+        self.dp, self.section = lax.axis_index("dp"), lax.axis_index("section")
+        self.n_dp = lax.axis_size("dp")
+        self.nz = self.n_dp // 2
+        self.z, self.x = self.dp // 2, lax.rem(self.dp, 2)
+        self.y, self.c = self.section // 2, lax.rem(self.section, 2)
+
+    def at(self, dz=0, x=None, y=None, c=None):
+        x = self.x if x is None else x
+        y = self.y if y is None else y
+        c = self.c if c is None else c
+        return ((self.z + dz) * 2 + x, y * 2 + c)
+
+    def to_x(self):
+        return self.at(x=1 - self.x)
+
+    def to_y(self):
+        return self.at(y=1 - self.y)
+
+    def to_c(self):
+        return self.at(c=1 - self.c)
+
+    def greet(self):
+        barrier = pltpu.get_barrier_semaphore()
+        peers = [self.to_c(), self.to_y()]
+        peers += [(lax.rem(self.dp + k, self.n_dp), self.section) for k in range(1, self.n_dp)]
+        for peer in peers:
+            pl.semaphore_signal(barrier, inc=1, device_id=peer, device_id_type=MESH)
+        pl.semaphore_wait(barrier, len(peers))
+
+
+class Links:
+    def __init__(self, sends, recvs):
+        self.sends, self.recvs, self.used = sends, recvs, 0
+
+    def copy(self, src, dst, peer):
+        i = self.used
+        self.used += 1
+        return pltpu.make_async_remote_copy(
+            src_ref=src, dst_ref=dst, send_sem=self.sends.at[i], recv_sem=self.recvs.at[i],
+            device_id=peer, device_id_type=MESH,
+        )
+
+
+HALF = D // 2
+LEFT, RIGHT = slice(0, HALF), slice(HALF, D)
+
+
+class Scatter:
+    def __init__(self, me, links, given, held, core, xa, yb, ya, xb, right, left):
+        self.me, self.held = me, held
+        self.core, self.xa, self.yb, self.ya, self.xb = core, xa, yb, ya, xb
+        self.right, self.left = right, left
+        x, y, c, nz = me.x, me.y, me.c, me.nz
+        every = slice(None)
+        cols_a, cols_b = pl.ds(0, HALF), pl.ds(HALF, HALF)
+        self.core_copy = links.copy(given, core, me.to_c())
+        self.xa_copy = links.copy(held.at[:, 1 - x, :, :, cols_a], xa, me.to_x())
+        self.yb_copy = links.copy(held.at[:, :, 1 - y, :, cols_b], yb, me.to_y())
+        self.ya_copy = links.copy(held.at[:, x, 1 - y, :, cols_a], ya, me.to_y())
+        self.xb_copy = links.copy(held.at[:, 1 - x, y, :, cols_b], xb, me.to_x())
+        self.r_copy, self.l_copy = {}, {}
+        for k in range(nz - 1):
+            d = nz - 1 - k
+            self.r_copy[d] = links.copy(held.at[d, x, y], right.at[d], me.at(dz=1))
+            self.l_copy[k] = links.copy(held.at[k, x, y], left.at[k], me.at(dz=-1))
+
+    def add(self, z, x, y, cols, value):
+        self.held[z, x, y, :, cols] = self.held[z, x, y, :, cols] + value
+
+    def start(self):
+        self.core_copy.start()
+
+    def first(self):
+        me, core = self.me, self.core
+        x, y = me.x, me.y
+        self.core_copy.wait_recv()
+
+        @pl.loop(0, me.nz)
+        def _(z):
+            for i in range(2):
+                self.add(z, 1 - x, i, LEFT, core[z, 1 - x, i, :, LEFT])
+
+        self.xa_copy.start()
+
+        @pl.loop(0, me.nz)
+        def _(z):
+            for i in range(2):
+                self.add(z, i, 1 - y, RIGHT, core[z, i, 1 - y, :, RIGHT])
+
+        self.yb_copy.start()
+
+        @pl.loop(0, me.nz)
+        def _(z):
+            for i in range(2):
+                self.add(z, x, i, LEFT, core[z, x, i, :, LEFT])
+                self.add(z, i, y, RIGHT, core[z, i, y, :, RIGHT])
+
+    def second(self):
+        me = self.me
+        x, y = me.x, me.y
+        self.xa_copy.wait_recv()
+
+        @pl.loop(0, me.nz)
+        def _(z):
+            self.add(z, x, 1 - y, LEFT, self.xa[z, 1 - y])
+
+        self.ya_copy.start()
+        self.yb_copy.wait_recv()
+
+        @pl.loop(0, me.nz)
+        def _(z):
+            self.add(z, 1 - x, y, RIGHT, self.yb[z, 1 - x])
+
+        self.xb_copy.start()
+
+        @pl.loop(0, me.nz)
+        def _(z):
+            self.add(z, x, y, LEFT, self.xa[z, y])
+            self.add(z, x, y, RIGHT, self.yb[z, x])
+
+    def third(self):
+        me = self.me
+        self.ya_copy.wait_recv()
+        self.xb_copy.wait_recv()
+
+        @pl.loop(0, me.nz)
+        def _(z):
+            self.add(z, me.x, me.y, LEFT, self.ya[z])
+            self.add(z, me.x, me.y, RIGHT, self.xb[z])
+
+    def along(self, k):
+        me, nz, z = self.me, self.me.nz, self.me.z
+        d = nz - 1 - k
+        every = slice(None)
+
+        @pl.when(z < d)
+        def _():
+            @pl.when(z > 0)
+            def _():
+                self.r_copy[d].wait_recv()
+                self.add(d, me.x, me.y, every, self.right[d])
+
+            self.r_copy[d].start()
+
+        @pl.when(z > k)
+        def _():
+            @pl.when(z < nz - 1)
+            def _():
+                self.l_copy[k].wait_recv()
+                self.add(k, me.x, me.y, every, self.left[k])
+
+            self.l_copy[k].start()
+
+    def finish(self, total):
+        me, nz, z = self.me, self.me.nz, self.me.z
+        for copy in (self.core_copy, self.xa_copy, self.yb_copy, self.ya_copy, self.xb_copy):
+            copy.wait_send()
+        total[...] = self.held[z, me.x, me.y].astype(F32)
+        for d in range(nz):
+            if d > 0:
+
+                @pl.when(z < d)
+                def _():
+                    self.r_copy[d].wait_send()
+
+                @pl.when(z == d)
+                def _():
+                    self.r_copy[d].wait_recv()
+                    total[...] += self.right[d].astype(F32)
+
+            if d < nz - 1:
+
+                @pl.when(z > d)
+                def _():
+                    self.l_copy[d].wait_send()
+
+                @pl.when(z == d)
+                def _():
+                    self.l_copy[d].wait_recv()
+                    total[...] += self.left[d].astype(F32)
+
+
+def scatter_buffers(nz, width):
+    shapes = [(nz, 2, 2, width, D)] * 2 + [(nz, 2, width, HALF)] * 2 + [(nz, width, HALF)] * 2
+    return shapes + [(nz, width, D)] * 2
+
+
+def scatter_copies(nz):
+    return 5 + 2 * (nz - 1)
+
+
+class Gather:
+    def __init__(self, me, links, wide, cols, all_wide, all_cols):
+        self.me, self.all_wide, self.all_cols = me, all_wide, all_cols
+        self.wide, self.cols = wide, cols
+        span = cols.shape[-1] // me.n_dp
+        here = (me.dp, me.y, me.c)
+        self.first_copies = []
+        for k in range(1, me.n_dp):
+            peer = lax.rem(me.dp + k, me.n_dp)
+            part = pl.ds(pl.multiple_of(peer * span, 128), span)
+            self.first_copies.append(links.copy(wide, all_wide.at[here], (peer, me.section)))
+            self.first_copies.append(links.copy(cols.at[:, :, part], all_cols.at[here], (peer, me.section)))
+        across = (slice(None), me.y, me.c)
+        self.second_copies = [links.copy(a.at[across], a.at[across], me.to_y()) for a in (all_wide, all_cols)]
+        beside = (slice(None), slice(None), me.c)
+        self.third_copies = [links.copy(a.at[beside], a.at[beside], me.to_c()) for a in (all_wide, all_cols)]
+
+    def start(self):
+        me = self.me
+        span = self.cols.shape[-1] // me.n_dp
+        for copy in self.first_copies:
+            copy.start()
+        self.all_wide[me.dp, me.y, me.c] = self.wide[...]
+        part = pl.ds(pl.multiple_of(me.dp * span, 128), span)
+        self.all_cols[me.dp, me.y, me.c] = self.cols[:, :, part]
+
+    def second(self):
+        for copy in self.first_copies:
+            copy.wait()
+        for copy in self.second_copies:
+            copy.start()
+
+    def third(self):
+        for copy in self.second_copies:
+            copy.wait()
+        for copy in self.third_copies:
+            copy.start()
+
+    def finish(self):
+        for copy in self.third_copies:
+            copy.wait()
+
+
+class Total:
+    def __init__(self, me, links, acc, got):
+        self.acc, self.got, self.copies = acc, got, []
+        peers = [me.to_c(), me.to_y()]
+        step = 1
+        while step < me.n_dp:
+            bit = lax.rem(me.dp // step, 2)
+            peers.append((me.dp + step * (1 - 2 * bit), me.section))
+            step *= 2
+        for i, peer in enumerate(peers):
+            self.copies.append(links.copy(acc, got.at[i], peer))
+
+    def start(self, i):
+        self.copies[i].start()
+
+    def add(self, i):
+        self.copies[i].wait()
+        self.acc[...] += self.got[i]
+
+
+def pick_own(me, width):
+    def pick(v):
+        out = v[:, :width]
+        for s in range(1, 4):
+            out = jnp.where(me.section == s, v[:, s * width : (s + 1) * width], out)
+        return out
+
+    return pick
+
+
+def comm_kernel(dw, small, wide, cols, ga_o, gm_o, small_o, *scratch):
+    n_scatter = 8
+    sets = [scratch[i * n_scatter : (i + 1) * n_scatter] for i in range(3)]
+    all_wide, all_cols, got, total, sends, recvs, local = scratch[3 * n_scatter :]
+    me, links = Place(), Links(sends, recvs)
+    loads = []
+    for m in range(3):
+        loads.append(pltpu.make_async_copy(dw.at[m, :, :, :, me.c], sets[m][0], local.at[m]))
+        loads[m].start()
+    scat = [Scatter(me, links, dw.at[m, :, :, :, 1 - me.c], *sets[m]) for m in range(3)]
+    gather = Gather(me, links, wide, cols, all_wide, all_cols)
+    small_o[...] = small[...]
+    summed = Total(me, links, small_o, got)
+    me.greet()
+    for s in scat:
+        s.start()
+    gather.start()
+    summed.start(0)
+    for load in loads:
+        load.wait()
+    a, b, c = scat
+    a.first()
+    b.first()
+    summed.add(0)
+    summed.start(1)
+    a.second()
+    gather.second()
+    c.first()
+    summed.add(1)
+    summed.start(2)
+    a.third()
+    a.along(0)
+    b.second()
+    a.along(1)
+    gather.third()
+    b.third()
+    b.along(0)
+    a.along(2)
+    summed.add(2)
+    summed.start(3)
+    c.second()
+    b.along(1)
+    gather.finish()
+    width = total.shape[0]
+    rows = 16 * 4 * me.n_dp
+    wide_all = [all_wide[:, :, :, i].reshape(rows, D) for i in range(2)]
+    cols_all = [all_cols[:, :, :, i].reshape(rows, 4 * width) for i in range(2)]
+    cls_grads(wide_all, cols_all, ga_o, gm_o, pick_own(me, width))
+    c.third()
+    c.along(0)
+    b.along(2)
+    a.finish(total)
+    ga_o[0] = total[...].T
+    summed.add(3)
+    summed.start(4)
+    c.along(1)
+    b.finish(total)
+    gm_o[0, 0] = total[...].T
+    c.along(2)
+    summed.add(4)
+    c.finish(total)
+    gm_o[0, 1] = total[...].T
+
+
+def combine(dw, small, wide, cols, n_dp):
+    nz, width = n_dp // 2, FF // (4 * n_dp)
+    dw = dw.reshape(3, nz, 2, 2, 2, width, D)
+    steps = 2 + (n_dp - 1).bit_length()
+    count = 3 * scatter_copies(nz) + 2 * (n_dp - 1) + 4 + steps
+    return pl.pallas_call(
+        comm_kernel,
+        out_shape=[
+            jax.ShapeDtypeStruct((2, D, width), F32),
+            jax.ShapeDtypeStruct((2, 2, D, width), F32),
+            jax.ShapeDtypeStruct(small.shape, F32),
+        ],
+        in_specs=[ANY, VM, VM, VM],
+        out_specs=[VM] * 3,
+        scratch_shapes=[pltpu.VMEM(s, BF) for s in scatter_buffers(nz, width) * 3]
+        + [
+            pltpu.VMEM((n_dp, 2, 2, 2, 16, D), BF),
+            pltpu.VMEM((n_dp, 2, 2, 2, 16, 4 * width), BF),
+            pltpu.VMEM((steps,) + small.shape, F32),
+            pltpu.VMEM((width, D), F32),
+            pltpu.SemaphoreType.DMA((count,)),
+            pltpu.SemaphoreType.DMA((count,)),
+            pltpu.SemaphoreType.DMA((3,)),
+        ],
+        compiler_params=pltpu.CompilerParams(
+            vmem_limit_bytes=56 * 2**20, collective_id=0, has_side_effects=True
+        ),
+    )(dw, small, wide, cols)
+
+
 def swap_half(v):
     size = lax.axis_size("section")
     per_micro = size // MICRO
@@ -521,15 +891,21 @@
     fourth, dlead, cols, wide, small1 = cls_chain(
         cls, swap_half(cls), cls_cot, cls_cot_other, counts, aw, ab, an, mw, mb, ms, embed
     )
-    cols = lax.all_to_all(cols, BOTH, split_axis=2, concat_axis=1, tiled=True)
-    wide = lax.all_gather(wide, BOTH, axis=1, tiled=True)
     encoded = second.reshape(OWN, SEG, D).at[:, 0].set(fourth[:OWN].astype(BF)).reshape(ROWS, D)
     dx, dw, small0 = backward(
         cot, dlead, tokens, n1, rs1, n2, rs2, first, qkv, p, ctx, act, gp, aw, an, mw, ms
     )
-    red = lax.psum_scatter(dw, BOTH, scatter_dimension=1, tiled=True)
-    small = lax.psum(jnp.concatenate([small0, small1], axis=0), BOTH)
-    ga, gm = place(red, cols, wide)
+    small = jnp.concatenate([small0, small1], axis=0)
+    n_dp, n_section = lax.axis_size("dp"), lax.axis_size("section")
+    width = FF // (n_dp * n_section)
+    if n_section == 4 and n_dp & (n_dp - 1) == 0 and width % 16 == 0 and 4 * width % 128 == 0:
+        ga, gm, small = combine(dw, small, wide, cols, n_dp)
+    else:
+        cols = lax.all_to_all(cols, BOTH, split_axis=2, concat_axis=1, tiled=True)
+        wide = lax.all_gather(wide, BOTH, axis=1, tiled=True)
+        red = lax.psum_scatter(dw, BOTH, scatter_dimension=1, tiled=True)
+        small = lax.psum(small, BOTH)
+        ga, gm = place(red, cols, wide)
     return (
         encoded,
         dx,

time: 489 us -> 246 us (0.50)
  waiting for transfers between devices: 321 us -> 1.14 us
  Pallas kernels: 110 us -> 223 us
  local copies, waits for them, and re-layouts: 29.7 us -> 14.6 us
  between operations: 14.1 us -> 0.99 us
  starting transfers between devices: 7.77 us -> 0.64 us
    reduce_scatter x1 -> x0, waiting for transfers between devices: 168 us -> none  [on_device(): red = lax.psum_scatter(dw, BOTH, scatter_dimension=1, tiled=True)]
    pallas_call x1, Pallas kernels: 3.52 us -> 116 us  [combine(): pl.pallas_call(comm_kernel, out_shape=[jax.ShapeDtypeStruct((2, D, width)...]
    psum x1 -> x0, waiting for transfers between devices: 106 us -> none  [on_device(): small = lax.psum(jnp.concatenate([small0, small1], axis=0), BOTH)]
    all_gather x1 -> x0, waiting for transfers between devices: 43.5 us -> none  [on_device(): wide = lax.all_gather(wide, BOTH, axis=1, tiled=True)]
    unnamed x24 -> x22, local copies, waits for them, and re-layouts: 16.8 us -> 8.98 us
    all_to_all x1 -> x0, starting transfers between devices: 7.02 us -> none  [on_device(): cols = lax.all_to_all(cols, BOTH, split_axis=2, concat_axis=1, tiled=True)]
  transfers between devices with their start and end apart: 6 -> 2, of which waited for: 4 -> 1; matrix products, arithmetic and copies ran while one was open for 5% -> 0% of each run, Pallas kernels for 0% -> 0%
where the time goes in v2:
time: 246 us; the launch traced here: 243 us
  Pallas kernels  223 us (91%)
  local copies, waits for them, and re-layouts  14.6 us (6%)
  other arithmetic  2.71 us (1%)
    pallas_call x1, Pallas kernels, combine(): pl.pallas_call(comm_kernel, out_shape=[jax.ShapeDtypeStruct((2, D, width)...  116 us
    pallas_call x1, Pallas kernels, backward(): pl.pallas_call(bwd_kernel, out_shape=[jax.ShapeDtypeStruct(*s) for s in s...  54 us
    pallas_call x1, Pallas kernels, forward(): pl.pallas_call(fwd_kernel, out_shape=shapes, in_specs=[VM, ANY, VM, VM, A...  39.8 us
    pallas_call x1, Pallas kernels, cls_chain(): pl.pallas_call(cls_kernel, out_shape=[jax.ShapeDtypeStruct(*s) for s in s...  13 us
    unnamed x22, local copies, waits for them, and re-layouts  8.98 us
  transfers between devices with their start and end apart: 2, of which 1 were waited for; matrix products, arithmetic and copies ran while one was open for 0% of the time, Pallas kernels for 0%

profile of v2, /device:TPU:0, one launch (start us, length us, event | category | flops | bytes accessed | tf_op | source)
XLA Modules:
  0.0 242.9 jit_solution(12769262245846902813)
XLA Ops:
  0.6 1.3 copy.29.ab
  1.9 1.3 copy.30.ms
  3.2 39.8 %shard_map.169 = (bf16[768,768]{1,0:T(8,128)(2,1)}, bf16[768,768]{1,0:T(8,128)(2,1)}, bf16[768,768]{1,0:T(8,128)(2,1)}, f32[768,1]{1,0:T(8,128)}, bf16[768,768]{...) custom-call(bf16[768,768]{1,0:T(8,128)(2,1)} %x.3, ...), custom_call_target="tpu_custom_call" | custom-call | tf_op jit(solution)/shard_map/pallas_call | solution.py:201
  43.0 0.5 collective-permute-start
  43.6 0.9 slice.65
  44.5 0.0 copy-start.1
  44.5 0.1 collective-permute-start.1
  44.6 1.1 collective-permute-done.1.cother_ref
  45.8 0.6 copy-done.4
  46.4 13.0 %shard_map.170 = (f32[8,768]{1,0:T(8,128)}, f32[8,768]{1,0:T(8,128)}, bf16[2,16,3072]{2,1,0:T(8,128)(2,1)}, bf16[2,16,768]{2,1,0:T(8,128)(2,1)}, f32[20,768]{1,0:T(8,128)}) custom-call(f32[8,768]{1,0:T(8,128)} %get-tuple-element.45.own_ref, f32[8,768]{1,0:T(8,128)} %copy-done.3, f32[8,768]{1,0:T(8,128)} %copy-done.1, f32[8,768]{1,0:T(8,128)} %copy-done.4, ...), custom_call_target="tpu_custom_call" | custom-call | tf_op jit(solution)/shard_map/pallas_call | solution.py:338
  59.4 54.0 %shard_map.171 = (bf16[768,768]{1,0:T(8,128)(2,1)}, bf16[3,3072,768]{2,1,0:T(8,128)(2,1)}, f32[12,768]{1,0:T(8,128)}) custom-call(bf16[768,768]{1,0:T(8,128)(2,1)} %cot.1, f32[8,768]{1,0:T(8,128)} %get-tuple-element.47.dlead, bf16[768,768]{1,0:T(8,128)(2,1)} %x.3, bf16[768,768]{1,0:T(8,128)(2,1)} %get-tuple-element.48.n1_i, ...), custom_call_target="tpu_custom_call" | custom-call | tf_op jit(solution)/shard_map/pallas_call | solution.py:470
  113.4 1.5 pad_maximum_fusion.small
  114.8 116.1 %shard_map.172 = (f32[2,768,96]{2,1,0:T(8,128)}, f32[2,2,768,96]{3,2,1,0:T(8,128)}, f32[32,768]{1,0:T(8,128)}) custom-call(bf16[3,4,2,2,2,96,768]{6,5,4,3,2,1,0:T(8,128)(2,1)} %bitcast.29, f32[32,768]{1,0:T(8,128)} %pad_maximum_fusion.small, bf16[2,16,768]{2,1,0:T(8,128)(2,1)} %get-tuple-element.62.wide, bf16[2,16,3072]{2,1,0:T(8,128)(2,1)} %get-tuple-element.63.cols), custom_call_target="tpu_custom_call" | custom-call | tf_op jit(solution)/shard_map/pallas_call | solution.py:856
  230.9 0.9 slice_bitcast_fusion.1
  231.9 0.8 slice_bitcast_fusion.7
  232.7 0.8 slice_bitcast_fusion.3
  233.5 1.3 slice.64
  234.9 2.2 copy.36
  237.1 0.6 copy.37
  237.7 1.5 copy.38
  239.2 0.6 copy.39
  239.8 0.6 pad_maximum_fusion.4
  240.4 0.6 pad_maximum_fusion.2
  241.1 1.6 scatter.4
  (18 shorter events, 0.1 us)
Async XLA Ops:
  43.0 1.6 collective-permute-start
  44.5 1.3 copy-start.1
  44.5 1.3 collective-permute-start.1
  44.6 1.1 copy-start.3
  45.8 0.6 copy-start.4
  59.4 54.0 %copy-start.2 = (f32[20,768]{1,0:T(8,128)S(1)}, f32[20,768]{1,0:T(8,128)}, u32[]{:S(2)}) copy-start(f32[20,768]{1,0:T(8,128)} %get-tuple-element.61) | copy-start | bytes 184324
  114.8 120.0 %copy-start.5 = (f32[8,768]{1,0:T(8,128)S(1)}, f32[8,768]{1,0:T(8,128)}, u32[]{:S(2)}) copy-start(f32[8,768]{1,0:T(8,128)} %get-tuple-element.46) | copy-start | bytes 73732
  230.9 6.8 %copy-start = (f32[2,2,768,96]{3,2,1,0:T(8,128)S(1)}, f32[2,2,768,96]{3,2,1,0:T(8,128)}, u32[]{:S(2)}) copy-start(f32[2,2,768,96]{3,2,1,0:T(8,128)} %get-tuple-element.81) | copy-start | bytes 3538948

commit v3 on v2

v3 whole, which is shorter than its diff:
```python
import functools

import jax
import jax.numpy as jnp
from jax import lax
from jax.experimental import pallas as pl
from jax.experimental.pallas import tpu as pltpu
from jax.sharding import PartitionSpec as P

F32 = jnp.float32
BF = jnp.bfloat16
D = 768
FF = 3072
SEG = 128
HEAD = 64
HEADS = 12
PAIRS = 6
MICRO = 2
SEGS = 12
OWN = 6
ROWS = OWN * SEG
BLOCKS = (4, 2, 2, 2, 96, D)
BOTH = ("dp", "section")
MASKED = -1e30
VM = pl.BlockSpec(memory_space=pltpu.VMEM)
SM = pl.BlockSpec(memory_space=pltpu.SMEM)
ANY = pl.BlockSpec(memory_space=pl.ANY)
MESH = pl.DeviceIdType.MESH


def dot(a, b):
    return jnp.dot(a, b, preferred_element_type=F32)


def dot_nt(a, b):
    return lax.dot_general(a, b, (((1,), (1,)), ((), ())), preferred_element_type=F32)


def dot_tn(a, b):
    return lax.dot_general(a, b, (((0,), (0,)), ((), ())), preferred_element_type=F32)


def gelu_parts(h):
    e = jnp.exp(-0.5 * h * h)
    t = 1.0 / (1.0 + (0.3275911 * 0.7071067811865476) * jnp.abs(h))
    poly = t * (
        0.127414796
        + t * (-0.142248368 + t * (0.7107068705 + t * (-0.7265760135 + t * 0.5307027145)))
    )
    tail = poly * e
    phi = jnp.where(h >= 0.0, 1.0 - tail, tail)
    return h * phi, phi + h * (0.3989422804014327 * e)


def norm_rows(r):
    center = r - jnp.mean(r, axis=-1, keepdims=True)
    rstd = lax.rsqrt(jnp.mean(center * center, axis=-1, keepdims=True) + 1e-5)
    return center * rstd, rstd


def norm_back(dy, n, rstd, gain):
    dyg = dy * gain
    return (
        dyg
        - jnp.mean(dyg, axis=-1, keepdims=True)
        - n * jnp.mean(dyg * n, axis=-1, keepdims=True)
    ) * rstd


def halves(v):
    lane = lax.broadcasted_iota(jnp.int32, v.shape, 1)
    zero = jnp.zeros_like(v)
    return jnp.concatenate([jnp.where(lane < HEAD, v, zero), jnp.where(lane < HEAD, zero, v)], 0)


def unhalve(v):
    top, bottom = v[:SEG], v[SEG:]
    lane = lax.broadcasted_iota(jnp.int32, top.shape, 1)
    return jnp.where(lane < HEAD, top, bottom)


def fold8(v):
    return jnp.sum(v.reshape(v.shape[0] // 8, 8, v.shape[1]), axis=0)


def block(ref, j):
    return ref[j].reshape(D, D)


def row(ref, *idx):
    i = idx[-1]
    return ref[idx[:-1] + (slice(i, i + 1), slice(None))].astype(F32)


class Copies:
    def __init__(self, sems):
        self.sems, self.all = sems, []

    def start(self, src, dst):
        copy = pltpu.make_async_copy(src, dst, self.sems.at[len(self.all)])
        copy.start()
        self.all.append(copy)
        return copy


def fwd_kernel(
    x_ref, aw, ab, an, mw, mb, ms,
    second_o, first_o, n1_o, rs1_o, n2_o, rs2_o, qkv_o, p_o, ctx_o, act_o, gp_o, cls_o,
    wq, w1, w2, second, first, n1, rs1, n2, rs2, qkv, p, ctx, act, gp, r, wsem, osem,
):
    outs, loads = Copies(osem), Copies(wsem)
    for j in range(4):
        s = slice(j * D, (j + 1) * D)
        loads.start(aw.at[0, :, s], wq.at[:, s])
    loads.start(mw.at[0, 0], w1)
    loads.start(mw.at[0, 1], w2)
    loads = loads.all
    x = x_ref[...]
    for j in range(3):
        loads[j].wait()
        s = slice(j * D, (j + 1) * D)
        v = dot(x, wq[:, s])
        if j != 1:
            v = v + row(ab, 0, j // 2)
        qkv[:, s] = v.astype(BF)
    outs.start(qkv, qkv_o)

    @pl.loop(0, OWN)
    def _(g):
        rows = pl.ds(pl.multiple_of(g * SEG, SEG), SEG)
        for h in range(PAIRS):
            c = slice(h * 128, (h + 1) * 128)
            q = qkv[rows, c] * jnp.asarray(0.125, BF)
            kc = halves(qkv[rows, D + h * 128 : D + (h + 1) * 128])
            vc = halves(qkv[rows, 2 * D + h * 128 : 2 * D + (h + 1) * 128])
            s = dot_nt(q, kc)
            ps = []
            for i in range(2):
                si = s[:, i * 128 : (i + 1) * 128]
                e = jnp.exp(si - jnp.max(si, axis=-1, keepdims=True))
                ps.append((e / jnp.sum(e, axis=-1, keepdims=True)).astype(BF))
            pp = jnp.concatenate(ps, axis=1)
            p[pl.ds(pl.multiple_of(g * ROWS + h * SEG, SEG), SEG), :] = pp
            ctx[rows, c] = dot(pp, vc).astype(BF)

    outs.start(p, p_o)
    outs.start(ctx, ctx_o)
    loads[3].wait()
    r[...] = x.astype(F32) + dot(ctx[...], wq[:, 3 * D :]) + row(ab, 0, 2)

    @pl.loop(0, ROWS // 64)
    def _(i):
        rows = pl.ds(pl.multiple_of(i * 64, 64), 64)
        n, rs = norm_rows(r[rows, :])
        n1[rows, :] = n.astype(BF)
        rs1[rows, :] = rs
        first[rows, :] = (n * row(an, 0, 0) + row(an, 0, 1)).astype(BF)

    outs.start(n1, n1_o)
    outs.start(rs1, rs1_o)
    outs.start(first, first_o)
    loads[4].wait()
    for j in range(4):
        s = slice(j * D, (j + 1) * D)
        r[...] = dot(first[...], w1[:, s]) + mb[0:1, s].astype(F32)

        for b in range(8):

            @pl.loop(0, 3)
            def _(i):
                rows = pl.ds(pl.multiple_of(i * 32, 32), 32)
                a, g = gelu_parts(r[pl.ds(pl.multiple_of(b * 96 + i * 32, 32), 32), :])
                at = (j, b // 4, b // 2 % 2, b % 2, rows, slice(None))
                act[at] = a.astype(BF)
                gp[at] = g.astype(BF)

    outs.start(act, act_o)
    outs.start(gp, gp_o)
    loads[5].wait()
    r[...] = first[...].astype(F32) + row(ms, 0, 0)
    for j in range(4):
        r[...] += dot_nt(block(act, j), w2[:, j * D : (j + 1) * D])
    cls_o[...] = jnp.zeros_like(cls_o)

    @pl.loop(0, OWN)
    def _(g):
        for part in range(2):
            rows = pl.ds(pl.multiple_of(g * SEG + part * 64, 64), 64)
            n, rs = norm_rows(r[rows, :])
            n2[rows, :] = n.astype(BF)
            rs2[rows, :] = rs
            value = (n * row(ms, 0, 1) + row(ms, 0, 2)).astype(BF)
            second[rows, :] = value
            if part == 0:
                cls_o[pl.ds(g, 1), :] = value[0:1].astype(F32)

    outs.start(n2, n2_o)
    outs.start(rs2, rs2_o)
    outs.start(second, second_o)
    for copy in outs.all:
        copy.wait()


def forward(x, aw, ab, an, mw, mb, ms):
    def big(width, dt=BF):
        return ((ROWS, width), dt)

    specs = [big(D), big(D), big(D), big(1, F32), big(D), big(1, F32), big(3 * D)]
    specs += [((OWN * ROWS, 256), BF), big(D), (BLOCKS, BF), (BLOCKS, BF)]
    shapes = [jax.ShapeDtypeStruct(*s) for s in specs] + [jax.ShapeDtypeStruct((8, D), F32)]
    return pl.pallas_call(
        fwd_kernel,
        out_shape=shapes,
        in_specs=[VM, ANY, VM, VM, ANY, VM, VM],
        out_specs=[ANY] * len(specs) + [VM],
        scratch_shapes=[pltpu.VMEM((D, FF), BF)] * 3
        + [pltpu.VMEM(*s) for s in specs]
        + [
            pltpu.VMEM((ROWS, D), F32),
            pltpu.SemaphoreType.DMA((6,)),
            pltpu.SemaphoreType.DMA((len(specs),)),
        ],
        compiler_params=pltpu.CompilerParams(vmem_limit_bytes=56 * 2**20),
    )(x, aw, ab, an, mw, mb, ms)


def cls_kernel(
    own_ref, other_ref, cown_ref, cother_ref, counts, aw, ab, an, mw, mb, ms, embed,
    fourth_o, dlead_o, cols_o, wide_o, small_o,
    wq, w1, w2, wsem,
):
    loads = Copies(wsem)
    loads.start(aw.at[1], wq)
    loads.start(mw.at[1, 0], w1)
    loads.start(mw.at[1, 1], w2)
    loads = loads.all
    section = lax.axis_index("section")
    per_micro = lax.axis_size("section") // MICRO
    half = lax.rem(section, per_micro)
    micro = section // per_micro
    ends = [counts[micro, 0], counts[micro, 0] + counts[micro, 1]]

    def layout(shape, axis):
        r = lax.broadcasted_iota(jnp.int32, shape, axis)
        seg = jnp.where(r < 8, r, r - 2)
        valid = (r < 6) | ((r >= 8) & (r < 14))
        doc = jnp.where(seg >= ends[0], 1, 0) + jnp.where(seg >= ends[1], 1, 0)
        start = jnp.where(doc == 0, 0, jnp.where(doc == 1, ends[0], ends[1]))
        pos = jnp.where(valid, seg - start, -1)
        return jnp.where(valid, doc, jnp.where(r < 16, 100 + r, -1)), pos, valid

    def order(a_ref, b_ref):
        a, b = a_ref[...], b_ref[...]
        first = half == 0
        return jnp.concatenate([jnp.where(first, a, b), jnp.where(first, b, a)], axis=0)

    def mine(v):
        return jnp.where(half == 0, v[:8], v[8:])

    doc_q, pos, valid = layout((16, 128), 0)
    doc_k, _, _ = layout((16, 128), 1)
    allowed = jnp.concatenate([doc_q == doc_k] * HEADS, axis=0)
    lanes8 = lax.broadcasted_iota(jnp.int32, (16, 8), 1)
    onehot = (pos[:, :8] == lanes8).astype(BF)
    leaders = order(own_ref, other_ref) + dot(onehot, embed[...])
    low = leaders.astype(BF)
    lane = lax.broadcasted_iota(jnp.int32, (16, D), 1) // HEAD

    def stack(v):
        return jnp.concatenate([jnp.where(lane == h, v, jnp.zeros_like(v)) for h in range(HEADS)], 0)

    def unstack(v):
        total = jnp.where(lane == 0, v[:16], 0.0)
        for h in range(1, HEADS):
            total = total + jnp.where(lane == h, v[h * 16 : (h + 1) * 16], 0.0)
        return total

    def deep(v):
        return jnp.concatenate([v, jnp.zeros((112, D), BF)], axis=0)

    loads[0].wait()
    q = (dot(low, wq[:, :D]) + row(ab, 1, 0)).astype(BF)
    k = dot(low, wq[:, D : 2 * D]).astype(BF)
    v = (dot(low, wq[:, 2 * D : 3 * D]) + row(ab, 1, 1)).astype(BF)
    qs, kd, vd = stack(q), deep(k), deep(v)
    scores = jnp.where(allowed, dot_nt(qs, kd) * 0.125, MASKED)
    e = jnp.exp(scores - jnp.max(scores, axis=-1, keepdims=True))
    probs = e / jnp.sum(e, axis=-1, keepdims=True)
    probs_low = probs.astype(BF)
    ctx = unstack(dot(probs_low, vd)).astype(BF)
    n1, rs1 = norm_rows(leaders + dot(ctx, wq[:, 3 * D :]) + row(ab, 1, 2))
    third = (n1 * row(an, 1, 0) + row(an, 1, 1)).astype(BF)
    loads[1].wait()
    act, gp = gelu_parts(dot(third, w1[...]) + mb[1:2, :].astype(F32))
    act = act.astype(BF)
    loads[2].wait()
    n2, rs2 = norm_rows(third.astype(F32) + dot_nt(act, w2[...]) + row(ms, 1, 0))
    fourth_o[...] = mine(n2 * row(ms, 1, 1) + row(ms, 1, 2))

    dy = order(cown_ref, cother_ref)
    small_o[10:11, :] = jnp.sum(mine(dy * n2), axis=0, keepdims=True)
    small_o[11:12, :] = jnp.sum(mine(dy), axis=0, keepdims=True)
    dr = norm_back(dy, n2, rs2, row(ms, 1, 1))
    dbf = dr.astype(BF)
    small_o[9:10, :] = jnp.sum(mine(dbf.astype(F32)), axis=0, keepdims=True)
    dh = (dot(dbf, w2[...]) * gp).astype(BF)
    dh_mine = mine(dh.astype(F32))
    dh_sum = jnp.sum(dh_mine, axis=0, keepdims=True)
    for j in range(4):
        small_o[5 + j : 6 + j, :] = dh_sum[:, j * D : (j + 1) * D]
    dthird = (dr + dot_nt(dh, w1[...])).astype(BF).astype(F32)
    small_o[3:4, :] = jnp.sum(mine(dthird * n1), axis=0, keepdims=True)
    small_o[4:5, :] = jnp.sum(mine(dthird), axis=0, keepdims=True)
    dr = norm_back(dthird, n1, rs1, row(an, 1, 0))
    dba = dr.astype(BF)
    small_o[2:3, :] = jnp.sum(mine(dba.astype(F32)), axis=0, keepdims=True)
    dctx = stack(dot_nt(dba, wq[:, 3 * D :]).astype(BF))
    dp = dot_nt(dctx, vd)
    dv = dot_tn(probs_low, dctx)[:16].astype(BF)
    ds = (probs * (dp - jnp.sum(dp * probs, axis=-1, keepdims=True))).astype(BF)
    dq = (unstack(dot(ds, kd)) * 0.125).astype(BF)
    dk = (dot_tn(ds, qs)[:16] * 0.125).astype(BF)
    small_o[0:1, :] = jnp.sum(mine(dq.astype(F32)), axis=0, keepdims=True)
    small_o[1:2, :] = jnp.sum(mine(dv.astype(F32)), axis=0, keepdims=True)
    dlead = dr + dot_nt(dq, wq[:, :D]) + dot_nt(dk, wq[:, D : 2 * D])
    dlead = dlead + dot_nt(dv, wq[:, 2 * D : 3 * D])
    dlead_mine = mine(dlead)
    dlead_o[...] = dlead_mine
    pos_mine = jnp.where(half == 0, pos[:8], pos[8:])
    for i in range(8):
        hit = jnp.where(pos_mine[:, 0:1] == i, dlead_mine, 0.0)
        small_o[12 + i : 13 + i, :] = jnp.sum(hit, axis=0, keepdims=True)
    zeros = jnp.zeros((8, D), F32)

    def pack(top, bottom):
        return jnp.concatenate([top, bottom], axis=0).astype(BF)

    cols_o[0] = pack(dh_mine, mine(act.astype(F32)))
    for j, piece in enumerate((dq, dk, dv)):
        cols_o[1, :, j * D : (j + 1) * D] = pack(mine(piece.astype(F32)), zeros)
    cols_o[1, :, 3 * D :] = pack(zeros, mine(dba.astype(F32)))
    wide_o[0] = pack(mine(third.astype(F32)), mine(dbf.astype(F32)))
    wide_o[1] = pack(mine(low.astype(F32)), mine(ctx.astype(F32)))


def cls_chain(own, other, cown, cother, counts, aw, ab, an, mw, mb, ms, embed):
    shapes = [((8, D), F32), ((8, D), F32), ((2, 16, FF), BF), ((2, 16, D), BF), ((20, D), F32)]
    return pl.pallas_call(
        cls_kernel,
        out_shape=[jax.ShapeDtypeStruct(*s) for s in shapes],
        in_specs=[VM, VM, VM, VM, SM, ANY, VM, VM, ANY, VM, VM, VM],
        out_specs=[VM] * 5,
        scratch_shapes=[pltpu.VMEM((D, FF), BF)] * 3 + [pltpu.SemaphoreType.DMA((3,))],
        compiler_params=pltpu.CompilerParams(vmem_limit_bytes=56 * 2**20),
    )(own, other, cown, cother, counts, aw, ab, an, mw, mb, ms, embed)


def cls_grads(wide, cols, ga_o, gm_o, pick):
    w0, c0 = wide[0], cols[0]
    low = lax.rem(lax.broadcasted_iota(jnp.int32, c0.shape, 0), 16) < 8
    zero = jnp.zeros_like(c0)
    gm_o[1, 0] = dot_tn(w0, pick(jnp.where(low, c0, zero)))
    gm_o[1, 1] = dot_tn(w0, pick(jnp.where(low, zero, c0)))
    ga_o[1] = dot_tn(wide[1], pick(cols[1]))


def place_kernel(red, cols, wide, ga_o, gm_o):
    ga_o[0] = red[0].astype(F32).T
    gm_o[0, 0] = red[1].astype(F32).T
    gm_o[0, 1] = red[2].astype(F32).T
    cls_grads(wide, cols, ga_o, gm_o, lambda v: v)


def place(red, cols, wide):
    width = red.shape[1]
    return pl.pallas_call(
        place_kernel,
        out_shape=[
            jax.ShapeDtypeStruct((2, D, width), F32),
            jax.ShapeDtypeStruct((2, 2, D, width), F32),
        ],
        in_specs=[VM] * 3,
        out_specs=[VM] * 2,
        compiler_params=pltpu.CompilerParams(vmem_limit_bytes=56 * 2**20),
    )(red, cols, wide)


class Place:
    def __init__(self):
        self.dp, self.section = lax.axis_index("dp"), lax.axis_index("section")
        self.n_dp = lax.axis_size("dp")
        self.nz = self.n_dp // 2
        self.z, self.x = self.dp // 2, lax.rem(self.dp, 2)
        self.y, self.c = self.section // 2, lax.rem(self.section, 2)

    def at(self, dz=0, x=None, y=None, c=None):
        x = self.x if x is None else x
        y = self.y if y is None else y
        c = self.c if c is None else c
        return ((self.z + dz) * 2 + x, y * 2 + c)

    def to_x(self):
        return self.at(x=1 - self.x)

    def to_y(self):
        return self.at(y=1 - self.y)

    def to_c(self):
        return self.at(c=1 - self.c)

    def greet(self):
        barrier = pltpu.get_barrier_semaphore()
        peers = [self.to_c(), self.to_y()]
        peers += [(lax.rem(self.dp + k, self.n_dp), self.section) for k in range(1, self.n_dp)]
        for peer in peers:
            pl.semaphore_signal(barrier, inc=1, device_id=peer, device_id_type=MESH)
        pl.semaphore_wait(barrier, len(peers))


class Links:
    def __init__(self, sends, recvs):
        self.sends, self.recvs, self.used = sends, recvs, 0

    def copy(self, src, dst, peer):
        i = self.used
        self.used += 1
        return pltpu.make_async_remote_copy(
            src_ref=src, dst_ref=dst, send_sem=self.sends.at[i], recv_sem=self.recvs.at[i],
            device_id=peer, device_id_type=MESH,
        )


HALF = D // 2
LEFT, RIGHT = slice(0, HALF), slice(HALF, D)


class Scatter:
    def __init__(self, me, links, held, core, xa, yb, ya, xb, right, left):
        self.me, self.held = me, held
        self.core, self.xa, self.yb, self.ya, self.xb = core, xa, yb, ya, xb
        self.right, self.left = right, left
        x, y, c, nz = me.x, me.y, me.c, me.nz
        cols_a, cols_b = pl.ds(0, HALF), pl.ds(HALF, HALF)
        self.core_copy = links.copy(held.at[:, :, :, 1 - c], core, me.to_c())
        self.xa_copy = links.copy(held.at[:, 1 - x, :, c, :, cols_a], xa, me.to_x())
        self.yb_copy = links.copy(held.at[:, :, 1 - y, c, :, cols_b], yb, me.to_y())
        self.ya_copy = links.copy(held.at[:, x, 1 - y, c, :, cols_a], ya, me.to_y())
        self.xb_copy = links.copy(held.at[:, 1 - x, y, c, :, cols_b], xb, me.to_x())
        self.r_copy, self.l_copy = {}, {}
        for k in range(nz - 1):
            d = nz - 1 - k
            self.r_copy[d] = links.copy(held.at[d, x, y, c], right.at[d], me.at(dz=1))
            self.l_copy[k] = links.copy(held.at[k, x, y, c], left.at[k], me.at(dz=-1))

    def add(self, z, x, y, cols, value):
        c = self.me.c
        self.held[z, x, y, c, :, cols] = self.held[z, x, y, c, :, cols] + value

    def start(self):
        self.core_copy.start()

    def first(self):
        me, core = self.me, self.core
        x, y = me.x, me.y
        self.core_copy.wait_recv()

        @pl.loop(0, me.nz)
        def _(z):
            for i in range(2):
                self.add(z, 1 - x, i, LEFT, core[z, 1 - x, i, :, LEFT])

        self.xa_copy.start()

        @pl.loop(0, me.nz)
        def _(z):
            for i in range(2):
                self.add(z, i, 1 - y, RIGHT, core[z, i, 1 - y, :, RIGHT])

        self.yb_copy.start()

        @pl.loop(0, me.nz)
        def _(z):
            for i in range(2):
                self.add(z, x, i, LEFT, core[z, x, i, :, LEFT])
                self.add(z, i, y, RIGHT, core[z, i, y, :, RIGHT])

    def second(self):
        me = self.me
        x, y = me.x, me.y
        self.xa_copy.wait_recv()

        @pl.loop(0, me.nz)
        def _(z):
            self.add(z, x, 1 - y, LEFT, self.xa[z, 1 - y])

        self.ya_copy.start()
        self.yb_copy.wait_recv()

        @pl.loop(0, me.nz)
        def _(z):
            self.add(z, 1 - x, y, RIGHT, self.yb[z, 1 - x])

        self.xb_copy.start()

        @pl.loop(0, me.nz)
        def _(z):
            self.add(z, x, y, LEFT, self.xa[z, y])
            self.add(z, x, y, RIGHT, self.yb[z, x])

    def third(self):
        me = self.me
        self.ya_copy.wait_recv()
        self.xb_copy.wait_recv()

        @pl.loop(0, me.nz)
        def _(z):
            self.add(z, me.x, me.y, LEFT, self.ya[z])
            self.add(z, me.x, me.y, RIGHT, self.xb[z])

    def along(self, k):
        me, nz, z = self.me, self.me.nz, self.me.z
        d = nz - 1 - k
        every = slice(None)

        @pl.when(z < d)
        def _():
            @pl.when(z > 0)
            def _():
                self.r_copy[d].wait_recv()
                self.add(d, me.x, me.y, every, self.right[d])

            self.r_copy[d].start()

        @pl.when(z > k)
        def _():
            @pl.when(z < nz - 1)
            def _():
                self.l_copy[k].wait_recv()
                self.add(k, me.x, me.y, every, self.left[k])

            self.l_copy[k].start()

    def finish(self, total):
        me, nz, z = self.me, self.me.nz, self.me.z
        for copy in (self.core_copy, self.xa_copy, self.yb_copy, self.ya_copy, self.xb_copy):
            copy.wait_send()
        total[...] = self.held[z, me.x, me.y, me.c].astype(F32)
        for d in range(nz):
            if d > 0:

                @pl.when(z < d)
                def _():
                    self.r_copy[d].wait_send()

                @pl.when(z == d)
                def _():
                    self.r_copy[d].wait_recv()
                    total[...] += self.right[d].astype(F32)

            if d < nz - 1:

                @pl.when(z > d)
                def _():
                    self.l_copy[d].wait_send()

                @pl.when(z == d)
                def _():
                    self.l_copy[d].wait_recv()
                    total[...] += self.left[d].astype(F32)


def scatter_buffers(nz, width):
    shapes = [(nz, 2, 2, width, D)] + [(nz, 2, width, HALF)] * 2 + [(nz, width, HALF)] * 2
    return shapes + [(nz, width, D)] * 2


def scatter_copies(nz):
    return 5 + 2 * (nz - 1)


class Gather:
    def __init__(self, me, links, wide, cols, all_wide, all_cols):
        self.me, self.all_wide, self.all_cols = me, all_wide, all_cols
        self.wide, self.cols = wide, cols
        span = cols.shape[-1] // me.n_dp
        here = (me.dp, me.y, me.c)
        self.first_copies = []
        for k in range(1, me.n_dp):
            peer = lax.rem(me.dp + k, me.n_dp)
            part = pl.ds(pl.multiple_of(peer * span, 128), span)
            self.first_copies.append(links.copy(wide, all_wide.at[here], (peer, me.section)))
            self.first_copies.append(links.copy(cols.at[:, :, part], all_cols.at[here], (peer, me.section)))
        across = (slice(None), me.y, me.c)
        self.second_copies = [links.copy(a.at[across], a.at[across], me.to_y()) for a in (all_wide, all_cols)]
        beside = (slice(None), slice(None), me.c)
        self.third_copies = [links.copy(a.at[beside], a.at[beside], me.to_c()) for a in (all_wide, all_cols)]

    def start(self):
        me = self.me
        span = self.cols.shape[-1] // me.n_dp
        for copy in self.first_copies:
            copy.start()
        self.all_wide[me.dp, me.y, me.c] = self.wide[...]
        part = pl.ds(pl.multiple_of(me.dp * span, 128), span)
        self.all_cols[me.dp, me.y, me.c] = self.cols[:, :, part]

    def second(self):
        for copy in self.first_copies:
            copy.wait()
        for copy in self.second_copies:
            copy.start()

    def third(self):
        for copy in self.second_copies:
            copy.wait()
        for copy in self.third_copies:
            copy.start()

    def finish(self):
        for copy in self.third_copies:
            copy.wait()


class Total:
    def __init__(self, me, links, acc, got):
        self.acc, self.got, self.copies = acc, got, []
        peers = [me.to_c(), me.to_y()]
        step = 1
        while step < me.n_dp:
            bit = lax.rem(me.dp // step, 2)
            peers.append((me.dp + step * (1 - 2 * bit), me.section))
            step *= 2
        for i, peer in enumerate(peers):
            self.copies.append(links.copy(acc, got.at[i], peer))

    def start(self, i):
        self.copies[i].start()

    def add(self, i):
        self.copies[i].wait()
        self.acc[...] += self.got[i]


def pick_own(me, width):
    def pick(v):
        out = v[:, :width]
        for s in range(1, 4):
            out = jnp.where(me.section == s, v[:, s * width : (s + 1) * width], out)
        return out

    return pick


N_SET = 7


class Net:
    def __init__(self, mats, small, wide, cols, ga_o, gm_o, scratch):
        sets = [scratch[i * N_SET : (i + 1) * N_SET] for i in range(3)]
        all_wide, all_cols, got, self.total, sends, recvs = scratch[3 * N_SET :]
        self.me, self.ga, self.gm, self.small = Place(), ga_o, gm_o, small
        links = Links(sends, recvs)
        self.attn, self.win, self.wout = [Scatter(self.me, links, mats[m], *sets[m]) for m in range(3)]
        self.gather = Gather(self.me, links, wide, cols, all_wide, all_cols)
        self.summed = Total(self.me, links, small, got)

    def cls(self):
        self.gather.finish()
        width = self.total.shape[0]
        rows = 16 * 4 * self.me.n_dp
        wide = [self.gather.all_wide[:, :, :, i].reshape(rows, D) for i in range(2)]
        cols = [self.gather.all_cols[:, :, :, i].reshape(rows, 4 * width) for i in range(2)]
        cls_grads(wide, cols, self.ga, self.gm, pick_own(self.me, width))

    def place(self, which, out):
        which.finish(self.total)
        out[...] = self.total[...].T


def bwd_kernel(
    fused,
    cot, dlead, x, small1, wide, cols, n1_i, rs1_i, n2_i, rs2_i, first_i, qkv_i, p_i, ctx_i, act_i, gp_i,
    aw, an, mw, ms,
    *refs,
):
    if fused:
        dx_o, small_o, ga_o, gm_o = refs[:4]
        refs = refs[4:]
    else:
        dx_o, small_o, dw_o = refs[:3]
        refs = refs[3:]
    w1, w2, first, n1, rs1, n2, rs2, qkv, p, ctx, act, gp, dwout, r, db, sums, wsem, osem = refs[:18]
    loads = Copies(wsem)
    for src, dst in (
        (cot, dx_o), (n2_i, n2), (rs2_i, rs2), (act_i, act), (mw.at[0, 1], w2), (gp_i, gp), (first_i, first),
        (mw.at[0, 0], w1), (n1_i, n1), (rs1_i, rs1), (ctx_i, ctx), (qkv_i, qkv), (p_i, p),
    ):
        loads.start(src, dst)
    loads = loads.all
    mats = (gp, act, dwout)
    if fused:
        net = Net(mats, small_o, wide, cols, ga_o, gm_o, refs[18:])
        attn, win, wout, summed = net.attn, net.win, net.wout, net.summed
        net.me.greet()
        net.gather.start()
    else:
        outs = Copies(osem)
    sums[...] = jnp.zeros_like(sums)

    def norm_step(rows, dy, n_ref, rs_ref, gain, at):
        n = n_ref[rows, :].astype(F32)
        dr = norm_back(dy, n, rs_ref[rows, :], gain)
        r[rows, :] = dr
        low = dr.astype(BF)
        db[rows, :] = low
        sums[at] += fold8(low.astype(F32))
        sums[at + 1] += fold8(dy * n)
        sums[at + 2] += fold8(dy)

    def put(ref, j, value):
        ref[j] = value.astype(BF).reshape(BLOCKS[1:])

    def done(which):
        if fused:
            (attn, win, wout)[which].start()
        else:
            outs.start(mats[which], dw_o.at[which])

    for i in range(3):
        loads[i].wait()

    @pl.loop(0, OWN)
    def _(g):
        for part in range(2):
            rows = pl.ds(pl.multiple_of(g * SEG + part * 64, 64), 64)
            dy = dx_o[rows, :].astype(F32)
            if part == 0:
                cls = lax.broadcasted_iota(jnp.int32, (64, D), 0) == 0
                lead = dlead[pl.ds(g, 1), :].astype(BF).astype(F32)
                dy = jnp.where(cls, lead, dy)
            norm_step(rows, dy, n2, rs2, row(ms, 0, 1), 0)

    loads[3].wait()
    for j in range(4):
        put(dwout, j, dot_tn(block(act, j), db[...]))
    done(2)
    loads[4].wait()
    loads[5].wait()
    for j in range(4):
        low = (dot(db[...], w2[:, j * D : (j + 1) * D]) * block(gp, j).astype(F32)).astype(BF)
        put(gp, j, low)
        sums[6 + j] = fold8(low.astype(F32))
    load_wq = pltpu.make_async_copy(aw.at[0], w2, wsem.at[13])
    load_wq.start()
    if fused:
        wout.first()
    loads[6].wait()
    for j in range(4):
        put(act, j, dot_tn(block(gp, j), first[...]))
    done(1)
    if fused:
        net.gather.second()
    loads[7].wait()
    for j in range(4):
        r[...] += dot_nt(block(gp, j), w1[:, j * D : (j + 1) * D])
    if fused:
        win.first()
    loads[8].wait()
    loads[9].wait()

    @pl.loop(0, ROWS // 64)
    def _(i):
        rows = pl.ds(pl.multiple_of(i * 64, 64), 64)
        dy = r[rows, :].astype(BF).astype(F32)
        norm_step(rows, dy, n1, rs1, row(an, 0, 0), 3)

    loads[10].wait()
    put(gp, 3, dot_tn(db[...], ctx[...]))
    load_wq.wait()
    wq, dctx = w2, n2
    dctx[...] = dot_nt(db[...], wq[:, 3 * D :]).astype(BF)
    if fused:
        wout.second()
    loads[11].wait()
    loads[12].wait()

    def attention(g):
        rows = pl.ds(pl.multiple_of(g * SEG, SEG), SEG)
        for h in range(PAIRS):
            cq = slice(h * 128, (h + 1) * 128)
            ck = slice(D + h * 128, D + (h + 1) * 128)
            cv = slice(2 * D + h * 128, 2 * D + (h + 1) * 128)
            q = qkv[rows, cq]
            kc, vc = halves(qkv[rows, ck]), halves(qkv[rows, cv])
            dc = dctx[rows, cq]
            pp = p[pl.ds(pl.multiple_of(g * ROWS + h * SEG, SEG), SEG), :]
            dp = dot_nt(dc, vc)
            pf = pp.astype(F32)
            ds = []
            for i in range(2):
                c = slice(i * 128, (i + 1) * 128)
                pi, di = pf[:, c], dp[:, c]
                ds.append((pi * (di - jnp.sum(di * pi, axis=-1, keepdims=True))).astype(BF))
            ds = jnp.concatenate(ds, axis=1)
            qkv[rows, cq] = (dot(ds, kc) * 0.125).astype(BF)
            qkv[rows, ck] = (unhalve(dot_tn(ds, q)) * 0.125).astype(BF)
            qkv[rows, cv] = unhalve(dot_tn(pp, dc)).astype(BF)

    pl.loop(0, OWN // 2)(attention)
    if fused:
        net.gather.third()
        wout.third()
        wout.along(0)
    pl.loop(OWN // 2, OWN)(attention)
    if fused:
        win.second()
        wout.along(1)
    for j in range(3):
        s = slice(j * D, (j + 1) * D)
        put(gp, j, dot_tn(qkv[:, s], x[...]))
        if j != 1:
            sums[10 + j // 2] = fold8(qkv[:, s].astype(F32))
    done(0)
    for i, at in enumerate((10, 11, 3, 4, 5, 6, 7, 8, 9, 0, 1, 2)):
        small_o[i : i + 1, :] = jnp.sum(sums[at], axis=0, keepdims=True)
    small_o[12:, :] = small1[...]
    if fused:
        summed.start(0)
        wout.along(2)
        win.third()
        win.along(0)
    dx_o[...] = (r[...] + dot_nt(qkv[...], wq[:, : 3 * D])).astype(BF)
    if not fused:
        for copy in outs.all:
            copy.wait()
        return
    attn.first()
    win.along(1)
    summed.add(0)
    summed.start(1)
    net.cls()
    net.place(wout, gm_o.at[0, 1])
    win.along(2)
    summed.add(1)
    summed.start(2)
    attn.second()
    net.place(win, gm_o.at[0, 0])
    summed.add(2)
    summed.start(3)
    attn.third()
    attn.along(0)
    summed.add(3)
    summed.start(4)
    attn.along(1)
    attn.along(2)
    summed.add(4)
    net.place(attn, ga_o.at[0])


def backward(fused, n_dp, cot, dlead, x, small1, wide, cols, kept, aw, an, mw, ms):
    width = FF // (4 * n_dp)
    if fused:
        shapes = [((ROWS, D), BF), ((32, D), F32), ((2, D, width), F32), ((2, 2, D, width), F32)]
    else:
        shapes = [((ROWS, D), BF), ((32, D), F32), ((3,) + BLOCKS, BF)]
    first, n1, rs1, n2, rs2, qkv, p, ctx, act, gp = kept
    scratch = [pltpu.VMEM((D, FF), BF)] * 2 + [pltpu.VMEM(a.shape, a.dtype) for a in kept]
    scratch += [
        pltpu.VMEM(BLOCKS, BF),
        pltpu.VMEM((ROWS, D), F32),
        pltpu.VMEM((ROWS, D), BF),
        pltpu.VMEM((12, 8, D), F32),
        pltpu.SemaphoreType.DMA((14,)),
        pltpu.SemaphoreType.DMA((3,)),
    ]
    params = {}
    if fused:
        steps = 2 + (n_dp - 1).bit_length()
        count = 3 * scatter_copies(n_dp // 2) + 2 * (n_dp - 1) + 4 + steps
        scratch += [pltpu.VMEM(s, BF) for s in scatter_buffers(n_dp // 2, width) * 3]
        scratch += [
            pltpu.VMEM((n_dp, 2, 2, 2, 16, D), BF),
            pltpu.VMEM((n_dp, 2, 2, 2, 16, 4 * width), BF),
            pltpu.VMEM((steps, 32, D), F32),
            pltpu.VMEM((width, D), F32),
            pltpu.SemaphoreType.DMA((count,)),
            pltpu.SemaphoreType.DMA((count,)),
        ]
        params = dict(collective_id=0, has_side_effects=True)
    return pl.pallas_call(
        functools.partial(bwd_kernel, fused),
        out_shape=[jax.ShapeDtypeStruct(*s) for s in shapes],
        in_specs=[ANY, VM, VM, VM, VM, VM] + [ANY] * 11 + [VM, ANY, VM],
        out_specs=[VM] * 4 if fused else [VM, VM, ANY],
        scratch_shapes=scratch,
        compiler_params=pltpu.CompilerParams(vmem_limit_bytes=63 * 2**20, **params),
    )(cot, dlead, x, small1, wide, cols, n1, rs1, n2, rs2, first, qkv, p, ctx, act, gp, aw, an, mw, ms)


def swap_half(v):
    size = lax.axis_size("section")
    per_micro = size // MICRO
    return lax.ppermute(v, "section", [(i, i - i % per_micro + (i + 1) % per_micro) for i in range(size)])


def on_device(tokens, counts, aw, ab, an, mw, mb, ms, embed, cot):
    cls_cot = jnp.pad(cot.reshape(OWN, SEG, D)[:, 0].astype(F32), ((0, 2), (0, 0)))
    cls_cot_other = swap_half(cls_cot)
    second, first, n1, rs1, n2, rs2, qkv, p, ctx, act, gp, cls = forward(tokens, aw, ab, an, mw, mb, ms)
    fourth, dlead, cols, wide, small1 = cls_chain(
        cls, swap_half(cls), cls_cot, cls_cot_other, counts, aw, ab, an, mw, mb, ms, embed
    )
    encoded = second.reshape(OWN, SEG, D).at[:, 0].set(fourth[:OWN].astype(BF)).reshape(ROWS, D)
    n_dp, n_section = lax.axis_size("dp"), lax.axis_size("section")
    kept = (first, n1, rs1, n2, rs2, qkv, p, ctx, act, gp)
    args = (cot, dlead, tokens, small1, wide, cols, kept, aw, an, mw, ms)
    if (n_dp // 2, 2, 2, 2, FF // (n_dp * n_section), D) == BLOCKS and n_section == 4:
        dx, small, ga, gm = backward(True, n_dp, *args)
    else:
        dx, small, dw = backward(False, n_dp, *args)
        cols = lax.all_to_all(cols, BOTH, split_axis=2, concat_axis=1, tiled=True)
        wide = lax.all_gather(wide, BOTH, axis=1, tiled=True)
        red = lax.psum_scatter(dw.reshape(3, FF, D), BOTH, scatter_dimension=1, tiled=True)
        small = lax.psum(small, BOTH)
        ga, gm = place(red, cols, wide)
    return (
        encoded,
        dx,
        ga,
        jnp.stack([small[0:3], small[12:15]]),
        jnp.stack([small[3:5], small[15:17]]),
        gm,
        jnp.stack([small[5:9].reshape(FF), small[17:21].reshape(FF)]),
        jnp.stack([small[9:12], small[21:24]]),
        small[24:32],
    )


def solution(mesh):
    return jax.shard_map(
        on_device,
        mesh=mesh,
        in_specs=(P(BOTH, None), P("dp", None)) + (P(),) * 7 + (P(BOTH, None),),
        out_specs=(
            P(BOTH, None),
            P(BOTH, None),
            P(None, None, BOTH),
            P(),
            P(),
            P(None, None, None, BOTH),
            P(),
            P(),
            P(),
        ),
        check_vma=False,
    )
```

time: 246 us -> 218 us (0.89)
  Pallas kernels: 223 us -> 195 us
    pallas_call x2 -> x1, Pallas kernels: 170 us -> 142 us  [backward(): pl.pallas_call(functools.partial(bwd_kernel, fused), out_shape=[jax.Shape...]
    unnamed x22 -> x23, local copies, waits for them, and re-layouts: 8.98 us -> 10 us
where the time goes in v3:
time: 218 us; the launch traced here: 214 us
  Pallas kernels  195 us (89%)
  local copies, waits for them, and re-layouts  15.6 us (7%)
    pallas_call x1, Pallas kernels, backward(): pl.pallas_call(functools.partial(bwd_kernel, fused), out_shape=[jax.Shape...  142 us
    pallas_call x1, Pallas kernels, forward(): pl.pallas_call(fwd_kernel, out_shape=shapes, in_specs=[VM, ANY, VM, VM, A...  39.7 us
    pallas_call x1, Pallas kernels, cls_chain(): pl.pallas_call(cls_kernel, out_shape=[jax.ShapeDtypeStruct(*s) for s in s...  13 us
    unnamed x23, local copies, waits for them, and re-layouts  10 us
  transfers between devices with their start and end apart: 2, of which 1 were waited for; matrix products, arithmetic and copies ran while one was open for 0% of the time, Pallas kernels for 0%

profile of v3, /device:TPU:0, one launch (start us, length us, event | category | flops | bytes accessed | tf_op | source)
XLA Modules:
  0.0 214.3 jit_solution(9048868348217163501)
XLA Ops:
  0.6 1.3 copy.29.ab
  1.9 1.3 copy.30.ms
  3.2 39.7 %shard_map.169 = (bf16[768,768]{1,0:T(8,128)(2,1)}, bf16[768,768]{1,0:T(8,128)(2,1)}, bf16[768,768]{1,0:T(8,128)(2,1)}, f32[768,1]{1,0:T(8,128)}, bf16[768,768]{...) custom-call(bf16[768,768]{1,0:T(8,128)(2,1)} %x.3, ...), custom_call_target="tpu_custom_call" | custom-call | tf_op jit(solution)/shard_map/pallas_call | solution.py:211
  43.0 0.5 collective-permute-start
  43.5 0.9 slice.65
  44.5 0.1 collective-permute-start.1
  44.6 0.0 collective-permute-done.other_ref
  44.6 1.1 collective-permute-done.1.cother_ref
  45.7 0.0 copy-done.3
  45.7 0.6 copy-done.4
  46.3 13.0 %shard_map.170 = (f32[8,768]{1,0:T(8,128)}, f32[8,768]{1,0:T(8,128)}, bf16[2,16,3072]{2,1,0:T(8,128)(2,1)}, bf16[2,16,768]{2,1,0:T(8,128)(2,1)}, f32[20,768]{1,0:T(8,128)}) custom-call(f32[8,768]{1,0:T(8,128)} %get-tuple-element.43.own_ref, f32[8,768]{1,0:T(8,128)} %copy-done.3, f32[8,768]{1,0:T(8,128)} %copy-done.2, f32[8,768]{1,0:T(8,128)} %copy-done.4, ...), custom_call_target="tpu_custom_call" | custom-call | tf_op jit(solution)/shard_map/pallas_call | solution.py:348
  59.3 142.1 %shard_map.171 = (bf16[768,768]{1,0:T(8,128)(2,1)}, f32[32,768]{1,0:T(8,128)}, f32[2,768,96]{2,1,0:T(8,128)}, f32[2,2,768,96]{3,2,1,0:T(8,128)}) custom-call(bf16[768,768]{1,0:T(8,128)(2,1)} %cot.1, f32[8,768]{1,0:T(8,128)} %get-tuple-element.45.dlead, bf16[768,768]{1,0:T(8,128)(2,1)} %x.3, f32[20,768]{1,0:T(8,128)} %get-tuple-element.46.small1, ...), custom_call_target="tpu_custom_call" | custom-call | tf_op jit(solution)/shard_map/pallas_call | solution.py:890
  201.4 0.9 slice_bitcast_fusion.1
  202.3 0.8 slice_bitcast_fusion.7
  203.2 0.8 slice_bitcast_fusion.3
  204.0 1.3 slice.64
  205.4 2.2 %copy.36 = f32[2,768,96]{1,2,0:T(8,128)} copy(f32[2,768,96]{2,1,0:T(8,128)} %get-tuple-element.74) | data formatting | bytes 1179648
  207.6 0.6 copy.37
  208.2 1.5 copy.38
  209.7 0.6 copy.39
  210.3 0.6 pad_maximum_fusion.3
  210.9 0.6 pad_maximum_fusion.1
  211.6 1.6 scatter.4
  213.1 1.0 copy.47
  (17 shorter events, 0.1 us)
Async XLA Ops:
  43.0 1.6 collective-permute-start
  44.5 1.3 copy-start.2
  44.5 1.3 collective-permute-start.1
  44.6 1.1 copy-start.3
  45.7 0.6 copy-start.4
  59.3 146.0 %copy-start.5 = (f32[8,768]{1,0:T(8,128)S(1)}, f32[8,768]{1,0:T(8,128)}, u32[]{:S(2)}) copy-start(f32[8,768]{1,0:T(8,128)} %get-tuple-element.44) | copy-start | bytes 73732
  201.4 6.8 %copy-start = (f32[2,2,768,96]{3,2,1,0:T(8,128)S(1)}, f32[2,2,768,96]{3,2,1,0:T(8,128)}, u32[]{:S(2)}) copy-start(f32[2,2,768,96]{3,2,1,0:T(8,128)} %get-tuple-element.77) | copy-start | bytes 3538948
  208.2 4.9 %copy-start.1 = (bf16[768,768]{1,0:T(8,128)(2,1)S(1)}, bf16[768,768]{1,0:T(8,128)(2,1)}, u32[]{:S(2)}) copy-start(bf16[768,768]{1,0:T(8,128)(2,1)} %get-tuple-element.101) | copy-start | bytes 3538948

commit v4 on v3

--- a/solution.py
+++ b/solution.py
@@ -421,11 +421,11 @@
     def __init__(self, sends, recvs):
         self.sends, self.recvs, self.used = sends, recvs, 0
 
-    def copy(self, src, dst, peer):
+    def copy(self, src, dst, peer, recv=None):
         i = self.used
         self.used += 1
         return pltpu.make_async_remote_copy(
-            src_ref=src, dst_ref=dst, send_sem=self.sends.at[i], recv_sem=self.recvs.at[i],
+            src_ref=src, dst_ref=dst, send_sem=self.sends.at[i], recv_sem=self.recvs.at[i] if recv is None else recv,
             device_id=peer, device_id_type=MESH,
         )
 
@@ -435,26 +435,24 @@
 
 
 class Scatter:
-    def __init__(self, me, links, held, core, xa, yb, ya, xb, right, left):
-        self.me, self.held = me, held
+    def __init__(self, me, links, held, core, xa, yb, ya, xb, zb, z_recv, j0, count):
+        self.me, self.held, self.js = me, held, range(j0, j0 + count)
         self.core, self.xa, self.yb, self.ya, self.xb = core, xa, yb, ya, xb
-        self.right, self.left = right, left
-        x, y, c, nz = me.x, me.y, me.c, me.nz
-        cols_a, cols_b = pl.ds(0, HALF), pl.ds(HALF, HALF)
-        self.core_copy = links.copy(held.at[:, :, :, 1 - c], core, me.to_c())
-        self.xa_copy = links.copy(held.at[:, 1 - x, :, c, :, cols_a], xa, me.to_x())
-        self.yb_copy = links.copy(held.at[:, :, 1 - y, c, :, cols_b], yb, me.to_y())
-        self.ya_copy = links.copy(held.at[:, x, 1 - y, c, :, cols_a], ya, me.to_y())
-        self.xb_copy = links.copy(held.at[:, 1 - x, y, c, :, cols_b], xb, me.to_x())
-        self.r_copy, self.l_copy = {}, {}
-        for k in range(nz - 1):
-            d = nz - 1 - k
-            self.r_copy[d] = links.copy(held.at[d, x, y, c], right.at[d], me.at(dz=1))
-            self.l_copy[k] = links.copy(held.at[k, x, y, c], left.at[k], me.at(dz=-1))
-
-    def add(self, z, x, y, cols, value):
+        x, y, c = me.x, me.y, me.c
+        js, cols_a, cols_b = pl.ds(j0, count), pl.ds(0, HALF), pl.ds(HALF, HALF)
+        self.core_copy = links.copy(held.at[js, :, :, 1 - c], core.at[js], me.to_c())
+        self.xa_copy = links.copy(held.at[js, 1 - x, :, c, :, cols_a], xa.at[js], me.to_x())
+        self.yb_copy = links.copy(held.at[js, :, 1 - y, c, :, cols_b], yb.at[js], me.to_y())
+        self.ya_copy = links.copy(held.at[js, x, 1 - y, c, :, cols_a], ya.at[js], me.to_y())
+        self.xb_copy = links.copy(held.at[js, 1 - x, y, c, :, cols_b], xb.at[js], me.to_x())
+        self.z_copies = [
+            links.copy(held.at[j, x, y, c], zb.at[me.z], (j * 2 + x, me.section), z_recv.at[me.z])
+            for j in self.js
+        ]
+
+    def add(self, j, x, y, cols, value):
         c = self.me.c
-        self.held[z, x, y, c, :, cols] = self.held[z, x, y, c, :, cols] + value
+        self.held[j, x, y, c, :, cols] = self.held[j, x, y, c, :, cols] + value
 
     def start(self):
         self.core_copy.start()
@@ -463,119 +461,84 @@
         me, core = self.me, self.core
         x, y = me.x, me.y
         self.core_copy.wait_recv()
-
-        @pl.loop(0, me.nz)
-        def _(z):
+        for j in self.js:
             for i in range(2):
-                self.add(z, 1 - x, i, LEFT, core[z, 1 - x, i, :, LEFT])
-
+                self.add(j, 1 - x, i, LEFT, core[j, 1 - x, i, :, LEFT])
         self.xa_copy.start()
-
-        @pl.loop(0, me.nz)
-        def _(z):
+        for j in self.js:
             for i in range(2):
-                self.add(z, i, 1 - y, RIGHT, core[z, i, 1 - y, :, RIGHT])
-
+                self.add(j, i, 1 - y, RIGHT, core[j, i, 1 - y, :, RIGHT])
         self.yb_copy.start()
-
-        @pl.loop(0, me.nz)
-        def _(z):
+        for j in self.js:
             for i in range(2):
-                self.add(z, x, i, LEFT, core[z, x, i, :, LEFT])
-                self.add(z, i, y, RIGHT, core[z, i, y, :, RIGHT])
+                self.add(j, x, i, LEFT, core[j, x, i, :, LEFT])
+                self.add(j, i, y, RIGHT, core[j, i, y, :, RIGHT])
 
     def second(self):
         me = self.me
         x, y = me.x, me.y
         self.xa_copy.wait_recv()
-
-        @pl.loop(0, me.nz)
-        def _(z):
-            self.add(z, x, 1 - y, LEFT, self.xa[z, 1 - y])
-
+        for j in self.js:
+            self.add(j, x, 1 - y, LEFT, self.xa[j, 1 - y])
         self.ya_copy.start()
         self.yb_copy.wait_recv()
-
-        @pl.loop(0, me.nz)
-        def _(z):
-            self.add(z, 1 - x, y, RIGHT, self.yb[z, 1 - x])
-
+        for j in self.js:
+            self.add(j, 1 - x, y, RIGHT, self.yb[j, 1 - x])
         self.xb_copy.start()
-
-        @pl.loop(0, me.nz)
-        def _(z):
-            self.add(z, x, y, LEFT, self.xa[z, y])
-            self.add(z, x, y, RIGHT, self.yb[z, x])
+        for j in self.js:
+            self.add(j, x, y, LEFT, self.xa[j, y])
+            self.add(j, x, y, RIGHT, self.yb[j, x])
 
     def third(self):
         me = self.me
         self.ya_copy.wait_recv()
         self.xb_copy.wait_recv()
-
-        @pl.loop(0, me.nz)
-        def _(z):
-            self.add(z, me.x, me.y, LEFT, self.ya[z])
-            self.add(z, me.x, me.y, RIGHT, self.xb[z])
-
-    def along(self, k):
-        me, nz, z = self.me, self.me.nz, self.me.z
-        d = nz - 1 - k
-        every = slice(None)
-
-        @pl.when(z < d)
-        def _():
-            @pl.when(z > 0)
+        for i, j in enumerate(self.js):
+            self.add(j, me.x, me.y, LEFT, self.ya[j])
+            self.add(j, me.x, me.y, RIGHT, self.xb[j])
+
+            @pl.when(me.z != j)
             def _():
-                self.r_copy[d].wait_recv()
-                self.add(d, me.x, me.y, every, self.right[d])
-
-            self.r_copy[d].start()
-
-        @pl.when(z > k)
-        def _():
-            @pl.when(z < nz - 1)
-            def _():
-                self.l_copy[k].wait_recv()
-                self.add(k, me.x, me.y, every, self.left[k])
-
-            self.l_copy[k].start()
-
-    def finish(self, total):
-        me, nz, z = self.me, self.me.nz, self.me.z
+                self.z_copies[i].start()
+
+    def drain(self):
         for copy in (self.core_copy, self.xa_copy, self.yb_copy, self.ya_copy, self.xb_copy):
             copy.wait_send()
-        total[...] = self.held[z, me.x, me.y, me.c].astype(F32)
-        for d in range(nz):
-            if d > 0:
-
-                @pl.when(z < d)
-                def _():
-                    self.r_copy[d].wait_send()
-
-                @pl.when(z == d)
-                def _():
-                    self.r_copy[d].wait_recv()
-                    total[...] += self.right[d].astype(F32)
-
-            if d < nz - 1:
-
-                @pl.when(z > d)
-                def _():
-                    self.l_copy[d].wait_send()
-
-                @pl.when(z == d)
-                def _():
-                    self.l_copy[d].wait_recv()
-                    total[...] += self.left[d].astype(F32)
+        for i, j in enumerate(self.js):
+
+            @pl.when(self.me.z != j)
+            def _():
+                self.z_copies[i].wait_send()
+
+
+class Matrix:
+    def __init__(self, me, links, z_recv, held, *buffers, cuts):
+        self.me, self.held, self.zb = me, held, buffers[-1]
+        self.units = [Scatter(me, links, held, *buffers, z_recv, j0, n) for j0, n in cuts]
+        self.arrivals = [
+            pltpu.make_async_remote_copy(
+                src_ref=self.zb.at[i], dst_ref=self.zb.at[i], send_sem=z_recv.at[i], recv_sem=z_recv.at[i],
+                device_id=(me.dp, me.section), device_id_type=MESH,
+            )
+            for i in range(me.nz)
+        ]
+
+    def finish(self, total):
+        me = self.me
+        for unit in self.units:
+            unit.drain()
+        total[...] = self.held[me.z, me.x, me.y, me.c].astype(F32)
+        for i in range(me.nz):
+
+            @pl.when(me.z != i)
+            def _():
+                self.arrivals[i].wait_recv()
+                total[...] += self.zb[i].astype(F32)
 
 
 def scatter_buffers(nz, width):
     shapes = [(nz, 2, 2, width, D)] + [(nz, 2, width, HALF)] * 2 + [(nz, width, HALF)] * 2
-    return shapes + [(nz, width, D)] * 2
-
-
-def scatter_copies(nz):
-    return 5 + 2 * (nz - 1)
+    return shapes + [(nz, width, D)]
 
 
 class Gather:
@@ -651,16 +614,19 @@
     return pick
 
 
-N_SET = 7
+N_SET = 6
+CUTS = (((0, 1), (1, 2), (3, 1)), ((0, 2), (2, 2)), ((0, 2), (2, 2)))
 
 
 class Net:
     def __init__(self, mats, small, wide, cols, ga_o, gm_o, scratch):
         sets = [scratch[i * N_SET : (i + 1) * N_SET] for i in range(3)]
-        all_wide, all_cols, got, self.total, sends, recvs = scratch[3 * N_SET :]
+        all_wide, all_cols, got, self.total, sends, recvs, z_recvs = scratch[3 * N_SET :]
         self.me, self.ga, self.gm, self.small = Place(), ga_o, gm_o, small
         links = Links(sends, recvs)
-        self.attn, self.win, self.wout = [Scatter(self.me, links, mats[m], *sets[m]) for m in range(3)]
+        self.attn, self.win, self.wout = [
+            Matrix(self.me, links, z_recvs.at[m], mats[m], *sets[m], cuts=CUTS[m]) for m in range(3)
+        ]
         self.gather = Gather(self.me, links, wide, cols, all_wide, all_cols)
         self.summed = Total(self.me, links, small, got)
 
@@ -700,7 +666,7 @@
     mats = (gp, act, dwout)
     if fused:
         net = Net(mats, small_o, wide, cols, ga_o, gm_o, refs[18:])
-        attn, win, wout, summed = net.attn, net.win, net.wout, net.summed
+        attn, win, wout, summed = net.attn.units, net.win.units, net.wout.units, net.summed
         net.me.greet()
         net.gather.start()
     else:
@@ -719,12 +685,6 @@
 
     def put(ref, j, value):
         ref[j] = value.astype(BF).reshape(BLOCKS[1:])
-
-    def done(which):
-        if fused:
-            (attn, win, wout)[which].start()
-        else:
-            outs.start(mats[which], dw_o.at[which])
 
     for i in range(3):
         loads[i].wait()
@@ -743,28 +703,33 @@
     loads[3].wait()
     for j in range(4):
         put(dwout, j, dot_tn(block(act, j), db[...]))
-    done(2)
+        if fused and j % 2 == 1:
+            wout[j // 2].start()
     loads[4].wait()
     loads[5].wait()
     for j in range(4):
         low = (dot(db[...], w2[:, j * D : (j + 1) * D]) * block(gp, j).astype(F32)).astype(BF)
         put(gp, j, low)
         sums[6 + j] = fold8(low.astype(F32))
+        if fused and j % 2 == 1:
+            wout[j // 2].first()
     load_wq = pltpu.make_async_copy(aw.at[0], w2, wsem.at[13])
     load_wq.start()
-    if fused:
-        wout.first()
     loads[6].wait()
     for j in range(4):
         put(act, j, dot_tn(block(gp, j), first[...]))
-    done(1)
-    if fused:
+        if fused and j % 2 == 1:
+            win[j // 2].start()
+    if fused:
+        wout[0].second()
+        win[0].first()
         net.gather.second()
     loads[7].wait()
     for j in range(4):
         r[...] += dot_nt(block(gp, j), w1[:, j * D : (j + 1) * D])
     if fused:
-        win.first()
+        wout[1].second()
+        win[1].first()
     loads[8].wait()
     loads[9].wait()
 
@@ -776,13 +741,17 @@
 
     loads[10].wait()
     put(gp, 3, dot_tn(db[...], ctx[...]))
+    if fused:
+        attn[2].start()
+        wout[0].third()
     load_wq.wait()
     wq, dctx = w2, n2
     dctx[...] = dot_nt(db[...], wq[:, 3 * D :]).astype(BF)
-    if fused:
-        wout.second()
     loads[11].wait()
     loads[12].wait()
+    if fused:
+        attn[2].first()
+        win[0].second()
 
     def attention(g):
         rows = pl.ds(pl.multiple_of(g * SEG, SEG), SEG)
@@ -808,53 +777,54 @@
 
     pl.loop(0, OWN // 2)(attention)
     if fused:
+        wout[1].third()
         net.gather.third()
-        wout.third()
-        wout.along(0)
     pl.loop(OWN // 2, OWN)(attention)
     if fused:
-        win.second()
-        wout.along(1)
-    for j in range(3):
+        win[1].second()
+        win[0].third()
+    for j in (1, 2, 0):
         s = slice(j * D, (j + 1) * D)
         put(gp, j, dot_tn(qkv[:, s], x[...]))
         if j != 1:
             sums[10 + j // 2] = fold8(qkv[:, s].astype(F32))
-    done(0)
+        if fused and j != 1:
+            attn[j // 2].start()
     for i, at in enumerate((10, 11, 3, 4, 5, 6, 7, 8, 9, 0, 1, 2)):
         small_o[i : i + 1, :] = jnp.sum(sums[at], axis=0, keepdims=True)
     small_o[12:, :] = small1[...]
     if fused:
         summed.start(0)
-        wout.along(2)
-        win.third()
-        win.along(0)
+        attn[1].first()
+        attn[0].first()
+        attn[2].second()
+    else:
+        for i in range(3):
+            outs.start(mats[i], dw_o.at[i])
     dx_o[...] = (r[...] + dot_nt(qkv[...], wq[:, : 3 * D])).astype(BF)
     if not fused:
         for copy in outs.all:
             copy.wait()
         return
-    attn.first()
-    win.along(1)
+    win[1].third()
     summed.add(0)
     summed.start(1)
     net.cls()
-    net.place(wout, gm_o.at[0, 1])
-    win.along(2)
+    net.place(net.wout, gm_o.at[0, 1])
+    attn[1].second()
+    attn[0].second()
     summed.add(1)
     summed.start(2)
-    attn.second()
-    net.place(win, gm_o.at[0, 0])
+    attn[2].third()
+    net.place(net.win, gm_o.at[0, 0])
     summed.add(2)
     summed.start(3)
-    attn.third()
-    attn.along(0)
+    attn[1].third()
+    attn[0].third()
     summed.add(3)
     summed.start(4)
-    attn.along(1)
-    attn.along(2)
     summed.add(4)
-    net.place(attn, ga_o.at[0])
+    net.place(net.attn, ga_o.at[0])
 
 
 def backward(fused, n_dp, cot, dlead, x, small1, wide, cols, kept, aw, an, mw, ms):
@@ -876,7 +846,7 @@
     params = {}
     if fused:
         steps = 2 + (n_dp - 1).bit_length()
-        count = 3 * scatter_copies(n_dp // 2) + 2 * (n_dp - 1) + 4 + steps
+        count = 5 * sum(len(cuts) for cuts in CUTS) + 3 * (n_dp // 2) + 2 * (n_dp - 1) + 4 + steps
         scratch += [pltpu.VMEM(s, BF) for s in scatter_buffers(n_dp // 2, width) * 3]
         scratch += [
             pltpu.VMEM((n_dp, 2, 2, 2, 16, D), BF),
@@ -885,6 +855,7 @@
             pltpu.VMEM((width, D), F32),
             pltpu.SemaphoreType.DMA((count,)),
             pltpu.SemaphoreType.DMA((count,)),
+            pltpu.SemaphoreType.DMA((3, n_dp // 2)),
         ]
         params = dict(collective_id=0, has_side_effects=True)
     return pl.pallas_call(

time: 218 us -> 189 us (0.87)
  the two profiles are of different devices: /device:TPU:0 before, /device:TPU:1 now
where the time goes in v4:
time: 189 us; the launch traced here: 186 us
  Pallas kernels  167 us (88%)
  local copies, waits for them, and re-layouts  15.6 us (8%)
    pallas_call x1, Pallas kernels, backward(): pl.pallas_call(functools.partial(bwd_kernel, fused), out_shape=[jax.Shape...  114 us
    pallas_call x1, Pallas kernels, forward(): pl.pallas_call(fwd_kernel, out_shape=shapes, in_specs=[VM, ANY, VM, VM, A...  39.8 us
    pallas_call x1, Pallas kernels, cls_chain(): pl.pallas_call(cls_kernel, out_shape=[jax.ShapeDtypeStruct(*s) for s in s...  13 us
    unnamed x23, local copies, waits for them, and re-layouts  10 us
  transfers between devices with their start and end apart: 2, of which 1 were waited for; matrix products, arithmetic and copies ran while one was open for 0% of the time, Pallas kernels for 0%

profile of v4, /device:TPU:1, one launch (start us, length us, event | category | flops | bytes accessed | tf_op | source)
XLA Modules:
  0.0 185.8 jit_solution(4187455394692355189)
XLA Ops:
  0.6 1.3 copy.29.ab
  1.9 1.3 copy.30.ms
  3.2 39.8 %shard_map.169 = (bf16[768,768]{1,0:T(8,128)(2,1)}, bf16[768,768]{1,0:T(8,128)(2,1)}, bf16[768,768]{1,0:T(8,128)(2,1)}, f32[768,1]{1,0:T(8,128)}, bf16[768,768]{...) custom-call(bf16[768,768]{1,0:T(8,128)(2,1)} %x.3, ...), custom_call_target="tpu_custom_call" | custom-call | tf_op jit(solution)/shard_map/pallas_call | solution.py:211
  43.1 0.1 collective-permute-start
  43.2 0.9 slice.65
  44.1 0.0 copy-start.2
  44.1 0.5 collective-permute-start.1
  44.6 0.0 collective-permute-done.other_ref
  44.6 0.8 collective-permute-done.1.cother_ref
  45.5 0.6 copy-done.4
  46.1 13.0 %shard_map.170 = (f32[8,768]{1,0:T(8,128)}, f32[8,768]{1,0:T(8,128)}, bf16[2,16,3072]{2,1,0:T(8,128)(2,1)}, bf16[2,16,768]{2,1,0:T(8,128)(2,1)}, f32[20,768]{1,0:T(8,128)}) custom-call(f32[8,768]{1,0:T(8,128)} %get-tuple-element.43.own_ref, f32[8,768]{1,0:T(8,128)} %copy-done.3, f32[8,768]{1,0:T(8,128)} %copy-done.2, f32[8,768]{1,0:T(8,128)} %copy-done.4, ...), custom_call_target="tpu_custom_call" | custom-call | tf_op jit(solution)/shard_map/pallas_call | solution.py:348
  59.1 113.7 %shard_map.171 = (bf16[768,768]{1,0:T(8,128)(2,1)}, f32[32,768]{1,0:T(8,128)}, f32[2,768,96]{2,1,0:T(8,128)}, f32[2,2,768,96]{3,2,1,0:T(8,128)}) custom-call(bf16[768,768]{1,0:T(8,128)(2,1)} %cot.1, f32[8,768]{1,0:T(8,128)} %get-tuple-element.45.dlead, bf16[768,768]{1,0:T(8,128)(2,1)} %x.3, f32[20,768]{1,0:T(8,128)} %get-tuple-element.46.small1, ...), custom_call_target="tpu_custom_call" | custom-call | tf_op jit(solution)/shard_map/pallas_call | solution.py:861
  172.8 0.9 slice_bitcast_fusion.1
  173.8 0.8 slice_bitcast_fusion.7
  174.6 0.8 slice_bitcast_fusion.3
  175.4 1.3 slice.64
  176.8 2.2 %copy.36 = f32[2,768,96]{1,2,0:T(8,128)} copy(f32[2,768,96]{2,1,0:T(8,128)} %get-tuple-element.74) | data formatting | bytes 1179648
  179.0 0.6 copy.37
  179.6 1.5 copy.38
  181.1 0.6 copy.39
  181.7 0.6 pad_maximum_fusion.3
  182.3 0.6 pad_maximum_fusion.1
  183.0 1.6 scatter.4
  184.6 1.0 copy.47
  (17 shorter events, 0.1 us)
Async XLA Ops:
  43.1 1.6 collective-permute-start
  44.1 1.4 copy-start.2
  44.1 1.4 collective-permute-start.1
  44.6 0.9 copy-start.3
  45.5 0.6 copy-start.4
  59.1 117.7 %copy-start.5 = (f32[8,768]{1,0:T(8,128)S(1)}, f32[8,768]{1,0:T(8,128)}, u32[]{:S(2)}) copy-start(f32[8,768]{1,0:T(8,128)} %get-tuple-element.44) | copy-start | bytes 73732
  172.8 6.8 %copy-start = (f32[2,2,768,96]{3,2,1,0:T(8,128)S(1)}, f32[2,2,768,96]{3,2,1,0:T(8,128)}, u32[]{:S(2)}) copy-start(f32[2,2,768,96]{3,2,1,0:T(8,128)} %get-tuple-element.77) | copy-start | bytes 3538948
  179.6 4.9 %copy-start.1 = (bf16[768,768]{1,0:T(8,128)(2,1)S(1)}, bf16[768,768]{1,0:T(8,128)(2,1)}, u32[]{:S(2)}) copy-start(bf16[768,768]{1,0:T(8,128)(2,1)} %get-tuple-element.101) | copy-start | bytes 3538948
